TPU v7x, 128 devices: a whole 4x4x4 slice. The times are simulated.
128 devices in a mesh: head: 8 (over x, core), code: 16 (over y, z).
Axes of the slice: x: 4, y: 4, z: 4, core: 2. Of those that a mesh axis runs over, the one named last changes fastest.
Arguments:
- tokens: bfloat16 [16384, 1024], P(('head', 'code')), may hold values from -128 to 128
- codebook: bfloat16 [8, 32768, 128], P('head', 'code'), may hold values from -12.5 to 12.5
- ema_counts: float32 [8, 32768], P('head', 'code'), may hold values from 0.5 to 4
- ema_sums: float32 [8, 32768, 128], P('head', 'code'), may hold values from -6 to 6
Outputs:
- quantized: bfloat16 [16384, 1024], P(('head', 'code'))
- new_counts: float32 [8, 32768], P('head', 'code')
- new_codebook: float32 [8, 32768, 128], P('head', 'code')
All inputs are finite; a program needn't handle non-finite values.
Results may differ from a plain program's by a relative error of at most 0.013.
Values may be sent and summed in bfloat16 or wider, within the bound.
A program may use at most 128 MiB of HBM per device.

v0:
```python
import jax
import jax.numpy as jnp
from jax import lax
from jax.sharding import PartitionSpec as P

sharpness = 0.25
momentum = 0.8


def shards(tokens, codebook, ema_counts, ema_sums):
    head_count = lax.axis_size("head")
    code_count = lax.axis_size("code")
    row_local = tokens.shape[0]
    head_width = codebook.shape[2]
    own_slices = lax.all_to_all(tokens, "head", split_axis=1, concat_axis=0, tiled=True)
    gathered = lax.all_gather(own_slices, "code", axis=0, tiled=True)
    grouped = gathered.reshape(code_count, head_count * row_local, head_width)
    centroids = codebook[0]
    code_norms = jnp.sum(jnp.square(centroids.astype(jnp.float32)), axis=1)
    block_rows = min(4096, code_count * head_count * row_local)
    sub_rows = block_rows // code_count
    block_total = head_count * row_local // sub_rows

    def advance(block_number, carried):
        assigned, numerators, quant_rows = carried
        block = lax.dynamic_slice_in_dim(grouped, block_number * sub_rows, sub_rows, 1)
        block = block.reshape(block_rows, head_width)
        products = jnp.einsum("rd,kd->rk", block, centroids, preferred_element_type=jnp.float32)
        logits = sharpness * (2.0 * products - code_norms[None, :])
        row_peak = lax.pmax(jnp.max(logits, axis=1), "code")
        exponent = jnp.exp(logits - row_peak[:, None])
        row_sums = lax.psum(jnp.sum(exponent, axis=1), "code")
        softmax_out = exponent / row_sums[:, None]
        weights = softmax_out.astype(jnp.bfloat16)
        assigned = assigned + jnp.sum(softmax_out, axis=0)
        numerators = numerators + jnp.einsum(
            "rk,rd->kd", weights, block, preferred_element_type=jnp.float32
        )
        partial_rows = jnp.dot(weights, centroids, preferred_element_type=jnp.float32)
        own_rows = lax.psum_scatter(
            partial_rows.astype(jnp.bfloat16), "code", scatter_dimension=0, tiled=True
        )
        quant_rows = lax.dynamic_update_slice_in_dim(
            quant_rows, own_rows, block_number * sub_rows, 0
        )
        return (assigned, numerators, quant_rows)

    start_state = (
        jnp.zeros((centroids.shape[0],), jnp.float32),
        jnp.zeros((centroids.shape[0], head_width), jnp.float32),
        jnp.zeros((head_count * row_local, head_width), jnp.bfloat16),
    )
    assigned, numerators, quant_rows = lax.fori_loop(0, block_total, advance, start_state)
    restored = lax.all_to_all(quant_rows, "head", split_axis=0, concat_axis=1, tiled=True)
    new_counts = momentum * ema_counts + (1.0 - momentum) * assigned[None, :]
    new_sums = momentum * ema_sums + (1.0 - momentum) * numerators[None, :, :]
    new_codebook = new_sums / new_counts[:, :, None]
    return (restored, new_counts, new_codebook)


def solution(mesh):
    placed = (
        P(("head", "code"), None),
        P("head", "code", None),
        P("head", "code"),
        P("head", "code", None),
    )
    return jax.shard_map(
        shards,
        mesh=mesh,
        in_specs=placed,
        out_specs=(P(("head", "code"), None), P("head", "code"), P("head", "code", None)),
        check_vma=False,
    )
```

profile of v0, /device:TPU:0, one launch (start us, length us, event | category | flops | bytes accessed | tf_op | source)
XLA Modules:
  0.0 1179.8 jit_solution(8047637211395061024)
XLA Ops:
  21.8 50.9 %all-gather.2.cloned.1.call-done = bf16[16384,128]{1,0:T(8,128)(2,1)} async-done(((bf16[1024,128]{1,0:T(8,128)(2,1)}), bf16[16384,128]{1,0:T(8,128)(2,1)}) %all-gather.2.cloned.1.call-update) | async-done | bytes 4194320 | tf_op jit(solution)/shard_map/all_gather | solution.py:16
  73.5 1086.9 %while.18 = (s32[]{:T(128)}, f32[2048]{0:T(1024)S(1)}, f32[2048,128]{1,0:T(8,128)}, bf16[1024,128]{1,0:T(8,128)(2,1)}, bf16[16,1024,128]{2,1,0:T(8,128)(2,1)}, /...) while((s32[]{:T(128)}, f32[2048]{0:T(1024)S(1)}, ...), condition=%wide.region_8.0_spmd.clone, body=%wide.region_1.0_spmd.clone.sunk | while | flops 6577719296 | bytes 232268048 | solution.py:53
  89.0 72.4 %pmax.13 = f32[4096]{0:T(1024)S(1)} all-reduce(f32[4096]{0:T(1024)S(1)} %get-tuple-element.227), channel_id=1, replica_groups=mesh['head'=8,'code'=16] {'code'}, use_global_device_ids=true, to_apply=%region_3.0 | all-reduce | flops 4096 | bytes 32768 | tf_op jit(solution)/shard_map/while/body/eval_jaxpr/pmax | solution.py:30
  161.4 14.9 %fusion.40 = f32[4096]{0:T(1024)S(1)} fusion(f32[4096,2048]{0,1:T(8,128)} %get-tuple-element.226, f32[4096]{0:T(1024)S(1)} %pmax.13, f32[2048]{0:T(1024)S(1)} %get-tuple-element.258), kind=kLoop, calls=%fused_computation.3.clone.1 | loop fusion | flops 41938944 | bytes 33595392 | tf_op jit(solution)/shard_map/while/body/eval_jaxpr/reduce_sum | solution.py:32
  176.3 69.7 %psum.13 = f32[4096]{0:T(1024)S(1)} all-reduce(f32[4096]{0:T(1024)S(1)} %fusion.40), channel_id=1, replica_groups=mesh['head'=8,'code'=16] {'code'}, use_global_device_ids=true, to_apply=%region_5.0 | all-reduce | flops 4096 | bytes 32768 | tf_op jit(solution)/shard_map/while/body/eval_jaxpr/psum | solution.py:32
  246.0 17.0 %fusion.41 = (f32[2048]{0:T(1024)S(1)}, bf16[4096,2048]{0,1:T(8,128)(2,1)S(1)}) fusion(f32[4096]{0:T(1024)S(1)} %psum.13, f32[4096]{0:T(1024)S(1)} %pmax.13, f32[2048]{0:T(1024)S(1)} %get-tuple-element.258, f32[4096,2048]{0,1:T(8,128)} %get-tuple-element.226), kind=kLoop, calls=%fused_computation.19.clone.1 | loop fusion | flops 58718208 | bytes 50380800 | tf_op jit(solution)/shard_map/while/body/eval_jaxpr/reduce_sum | solution.py:35
  283.8 60.3 %reduce-scatter.2.cloned.1.call-done = bf16[256,128]{1,0:T(8,128)(2,1)} async-done(((bf16[4096,128]{1,0:T(8,128)(2,1)}), bf16[256,128]{1,0:T(8,128)(2,1)}) %reduce-scatter.2.cloned.1.call-update) | async-done | bytes 65552 | tf_op jit(solution)/shard_map/while/body/eval_jaxpr/reduce_scatter | solution.py:40
  346.9 14.1 %fusion.39 = (f32[4096]{0:T(1024)S(1)}, f32[4096,2048]{0,1:T(8,128)}) fusion(f32[2048]{0:T(1024)S(1)} %get-tuple-element.258, bf16[4096,128]{1,0:T(8,128)(2,1)S(1)} %bitcast.38, bf16[2048,128]{1,0:T(8,128)(2,1)} %get-tuple-element.257), kind=kOutput, calls=%fused_computation.4.clone.1 | convolution fusion | flops 2181033984 | bytes 35151872 | tf_op jit(solution)/shard_map/while/body/eval_jaxpr/rd,kd->rk/dot_general | solution.py:28
  361.0 72.0 %pmax.13 = f32[4096]{0:T(1024)S(1)} all-reduce(f32[4096]{0:T(1024)S(1)} %get-tuple-element.227), channel_id=1, replica_groups=mesh['head'=8,'code'=16] {'code'}, use_global_device_ids=true, to_apply=%region_3.0 | all-reduce | flops 4096 | bytes 32768 | tf_op jit(solution)/shard_map/while/body/eval_jaxpr/pmax | solution.py:30
  433.0 14.9 %fusion.40 = f32[4096]{0:T(1024)S(1)} fusion(f32[4096,2048]{0,1:T(8,128)} %get-tuple-element.226, f32[4096]{0:T(1024)S(1)} %pmax.13, f32[2048]{0:T(1024)S(1)} %get-tuple-element.258), kind=kLoop, calls=%fused_computation.3.clone.1 | loop fusion | flops 41938944 | bytes 33595392 | tf_op jit(solution)/shard_map/while/body/eval_jaxpr/reduce_sum | solution.py:32
  448.0 69.7 %psum.13 = f32[4096]{0:T(1024)S(1)} all-reduce(f32[4096]{0:T(1024)S(1)} %fusion.40), channel_id=1, replica_groups=mesh['head'=8,'code'=16] {'code'}, use_global_device_ids=true, to_apply=%region_5.0 | all-reduce | flops 4096 | bytes 32768 | tf_op jit(solution)/shard_map/while/body/eval_jaxpr/psum | solution.py:32
  517.6 17.0 %fusion.41 = (f32[2048]{0:T(1024)S(1)}, bf16[4096,2048]{0,1:T(8,128)(2,1)S(1)}) fusion(f32[4096]{0:T(1024)S(1)} %psum.13, f32[4096]{0:T(1024)S(1)} %pmax.13, f32[2048]{0:T(1024)S(1)} %get-tuple-element.258, f32[4096,2048]{0,1:T(8,128)} %get-tuple-element.226), kind=kLoop, calls=%fused_computation.19.clone.1 | loop fusion | flops 58718208 | bytes 50380800 | tf_op jit(solution)/shard_map/while/body/eval_jaxpr/reduce_sum | solution.py:35
  555.8 59.9 %reduce-scatter.2.cloned.1.call-done = bf16[256,128]{1,0:T(8,128)(2,1)} async-done(((bf16[4096,128]{1,0:T(8,128)(2,1)}), bf16[256,128]{1,0:T(8,128)(2,1)}) %reduce-scatter.2.cloned.1.call-update) | async-done | bytes 65552 | tf_op jit(solution)/shard_map/while/body/eval_jaxpr/reduce_scatter | solution.py:40
  632.6 72.0 %pmax.13 = f32[4096]{0:T(1024)S(1)} all-reduce(f32[4096]{0:T(1024)S(1)} %get-tuple-element.227), channel_id=1, replica_groups=mesh['head'=8,'code'=16] {'code'}, use_global_device_ids=true, to_apply=%region_3.0 | all-reduce | flops 4096 | bytes 32768 | tf_op jit(solution)/shard_map/while/body/eval_jaxpr/pmax | solution.py:30
  704.6 14.9 %fusion.40 = f32[4096]{0:T(1024)S(1)} fusion(f32[4096,2048]{0,1:T(8,128)} %get-tuple-element.226, f32[4096]{0:T(1024)S(1)} %pmax.13, f32[2048]{0:T(1024)S(1)} %get-tuple-element.258), kind=kLoop, calls=%fused_computation.3.clone.1 | loop fusion | flops 41938944 | bytes 33595392 | tf_op jit(solution)/shard_map/while/body/eval_jaxpr/reduce_sum | solution.py:32
  719.6 69.7 %psum.13 = f32[4096]{0:T(1024)S(1)} all-reduce(f32[4096]{0:T(1024)S(1)} %fusion.40), channel_id=1, replica_groups=mesh['head'=8,'code'=16] {'code'}, use_global_device_ids=true, to_apply=%region_5.0 | all-reduce | flops 4096 | bytes 32768 | tf_op jit(solution)/shard_map/while/body/eval_jaxpr/psum | solution.py:32
  789.2 17.0 %fusion.41 = (f32[2048]{0:T(1024)S(1)}, bf16[4096,2048]{0,1:T(8,128)(2,1)S(1)}) fusion(f32[4096]{0:T(1024)S(1)} %psum.13, f32[4096]{0:T(1024)S(1)} %pmax.13, f32[2048]{0:T(1024)S(1)} %get-tuple-element.258, f32[4096,2048]{0,1:T(8,128)} %get-tuple-element.226), kind=kLoop, calls=%fused_computation.19.clone.1 | loop fusion | flops 58718208 | bytes 50380800 | tf_op jit(solution)/shard_map/while/body/eval_jaxpr/reduce_sum | solution.py:35
  827.4 59.9 %reduce-scatter.2.cloned.1.call-done = bf16[256,128]{1,0:T(8,128)(2,1)} async-done(((bf16[4096,128]{1,0:T(8,128)(2,1)}), bf16[256,128]{1,0:T(8,128)(2,1)}) %reduce-scatter.2.cloned.1.call-update) | async-done | bytes 65552 | tf_op jit(solution)/shard_map/while/body/eval_jaxpr/reduce_scatter | solution.py:40
  890.1 14.1 %fusion.39 = (f32[4096]{0:T(1024)S(1)}, f32[4096,2048]{0,1:T(8,128)}) fusion(f32[2048]{0:T(1024)S(1)} %get-tuple-element.258, bf16[4096,128]{1,0:T(8,128)(2,1)S(1)} %bitcast.38, bf16[2048,128]{1,0:T(8,128)(2,1)} %get-tuple-element.257), kind=kOutput, calls=%fused_computation.4.clone.1 | convolution fusion | flops 2181033984 | bytes 35151872 | tf_op jit(solution)/shard_map/while/body/eval_jaxpr/rd,kd->rk/dot_general | solution.py:28
  904.2 72.0 %pmax.13 = f32[4096]{0:T(1024)S(1)} all-reduce(f32[4096]{0:T(1024)S(1)} %get-tuple-element.227), channel_id=1, replica_groups=mesh['head'=8,'code'=16] {'code'}, use_global_device_ids=true, to_apply=%region_3.0 | all-reduce | flops 4096 | bytes 32768 | tf_op jit(solution)/shard_map/while/body/eval_jaxpr/pmax | solution.py:30
  976.2 14.9 %fusion.40 = f32[4096]{0:T(1024)S(1)} fusion(f32[4096,2048]{0,1:T(8,128)} %get-tuple-element.226, f32[4096]{0:T(1024)S(1)} %pmax.13, f32[2048]{0:T(1024)S(1)} %get-tuple-element.258), kind=kLoop, calls=%fused_computation.3.clone.1 | loop fusion | flops 41938944 | bytes 33595392 | tf_op jit(solution)/shard_map/while/body/eval_jaxpr/reduce_sum | solution.py:32
  991.2 69.7 %psum.13 = f32[4096]{0:T(1024)S(1)} all-reduce(f32[4096]{0:T(1024)S(1)} %fusion.40), channel_id=1, replica_groups=mesh['head'=8,'code'=16] {'code'}, use_global_device_ids=true, to_apply=%region_5.0 | all-reduce | flops 4096 | bytes 32768 | tf_op jit(solution)/shard_map/while/body/eval_jaxpr/psum | solution.py:32
  1060.8 17.0 %fusion.41 = (f32[2048]{0:T(1024)S(1)}, bf16[4096,2048]{0,1:T(8,128)(2,1)S(1)}) fusion(f32[4096]{0:T(1024)S(1)} %psum.13, f32[4096]{0:T(1024)S(1)} %pmax.13, f32[2048]{0:T(1024)S(1)} %get-tuple-element.258, f32[4096,2048]{0,1:T(8,128)} %get-tuple-element.226), kind=kLoop, calls=%fused_computation.19.clone.1 | loop fusion | flops 58718208 | bytes 50380800 | tf_op jit(solution)/shard_map/while/body/eval_jaxpr/reduce_sum | solution.py:35
  1099.0 60.0 %reduce-scatter.2.cloned.1.call-done = bf16[256,128]{1,0:T(8,128)(2,1)} async-done(((bf16[4096,128]{1,0:T(8,128)(2,1)}), bf16[256,128]{1,0:T(8,128)(2,1)}) %reduce-scatter.2.cloned.1.call-update) | async-done | bytes 65552 | tf_op jit(solution)/shard_map/while/body/eval_jaxpr/reduce_scatter | solution.py:40
  (68 shorter events, 151.8 us)
Async XLA Ops:
  7.2 65.6 %all-gather.2.cloned.1.call-start = ((), (), s32[]{:S(2)}) async-start(), calls=%async_computation.3 | async-start | bytes 4456448 | tf_op jit(solution)/shard_map/all_gather | solution.py:16
  73.5 1091.2 %copy-start.4 = (f32[1,2048]{1,0:T(1,128)S(1)}, f32[1,2048]{1,0:T(1,128)}, u32[]{:S(2)}) copy-start(f32[1,2048]{1,0:T(1,128)} %param.8) | copy-start | bytes 24580
  73.5 1091.2 %copy-start.2 = (f32[1,2048,128]{2,1,0:T(8,128)S(1)}, f32[1,2048,128]{2,1,0:T(8,128)}, u32[]{:S(2)}) copy-start(f32[1,2048,128]{2,1,0:T(8,128)} %param.9) | copy-start | bytes 3145732
  73.5 270.6 %reduce-scatter.2.cloned.1.call-start = ((), (), s32[]{:S(2)}) async-start(), calls=%async_computation.4 | async-start | bytes 1114112 | tf_op jit(solution)/shard_map/while/body/eval_jaxpr/reduce_scatter | solution.py:40
  176.3 92.4 %copy-start.1 = (bf16[2048,128]{1,0:T(8,128)(2,1)S(1)}, bf16[2048,128]{1,0:T(8,128)(2,1)}, u32[]{:S(2)}) copy-start(bf16[2048,128]{1,0:T(8,128)(2,1)} %get-tuple-element.257) | copy-start | bytes 1572868 | tf_op jit(solution)/shard_map/while
  262.9 5.7 copy-start
  345.6 270.1 %reduce-scatter.2.cloned.1.call-start = ((), (), s32[]{:S(2)}) async-start(), calls=%async_computation.4 | async-start | bytes 1114112 | tf_op jit(solution)/shard_map/while/body/eval_jaxpr/reduce_scatter | solution.py:40
  448.0 92.4 %copy-start.1 = (bf16[2048,128]{1,0:T(8,128)(2,1)S(1)}, bf16[2048,128]{1,0:T(8,128)(2,1)}, u32[]{:S(2)}) copy-start(bf16[2048,128]{1,0:T(8,128)(2,1)} %get-tuple-element.257) | copy-start | bytes 1572868 | tf_op jit(solution)/shard_map/while
  534.6 5.7 copy-start
  617.2 270.1 %reduce-scatter.2.cloned.1.call-start = ((), (), s32[]{:S(2)}) async-start(), calls=%async_computation.4 | async-start | bytes 1114112 | tf_op jit(solution)/shard_map/while/body/eval_jaxpr/reduce_scatter | solution.py:40
  719.6 92.4 %copy-start.1 = (bf16[2048,128]{1,0:T(8,128)(2,1)S(1)}, bf16[2048,128]{1,0:T(8,128)(2,1)}, u32[]{:S(2)}) copy-start(bf16[2048,128]{1,0:T(8,128)(2,1)} %get-tuple-element.257) | copy-start | bytes 1572868 | tf_op jit(solution)/shard_map/while
  806.2 5.7 copy-start
  888.8 270.2 %reduce-scatter.2.cloned.1.call-start = ((), (), s32[]{:S(2)}) async-start(), calls=%async_computation.4 | async-start | bytes 1114112 | tf_op jit(solution)/shard_map/while/body/eval_jaxpr/reduce_scatter | solution.py:40
  991.2 92.4 %copy-start.1 = (bf16[2048,128]{1,0:T(8,128)(2,1)S(1)}, bf16[2048,128]{1,0:T(8,128)(2,1)}, u32[]{:S(2)}) copy-start(bf16[2048,128]{1,0:T(8,128)(2,1)} %get-tuple-element.257) | copy-start | bytes 1572868 | tf_op jit(solution)/shard_map/while
  1077.8 5.7 copy-start
  1160.4 11.8 all-to-all-start.1
  1164.7 8.6 copy-start.3
Sparse Core Ops, SparseCore 0:
  20.5 52.1 all-gather.1
  274.7 69.3 reduce-scatter.1
  546.3 69.3 reduce-scatter.1
  817.9 69.3 reduce-scatter.1
  1089.5 69.3 reduce-scatter.1
where the time goes:
time: 1180 us
  blocking collectives  579 us (49%)
  waiting for transfers between devices  296 us (25%)
  other arithmetic  131 us (11%)
  matrix products  118 us (10%)
  local copies, waits for them, and re-layouts  37.1 us (3%)
  between operations  13.8 us (1%)
    pmax x4, blocking collectives, advance(): row_peak = lax.pmax(jnp.max(logits, axis=1), 'code')  289 us
    psum x4, blocking collectives, advance(): row_sums = lax.psum(jnp.sum(exponent, axis=1), 'code')  279 us
    reduce_scatter x4, waiting for transfers between devices, advance(): lax.psum_scatter(partial_rows.astype(jnp.bfloat16), 'code', scatter_dimen...  240 us
    reduce_sum x4, other arithmetic, advance(): assigned = assigned + jnp.sum(softmax_out, axis=0)  67.9 us
    reduce_sum x4, other arithmetic, advance(): row_sums = lax.psum(jnp.sum(exponent, axis=1), 'code')  59.6 us
    dot_general x4, matrix products, advance(): jnp.einsum('rd,kd->rk', block, centroids, preferred_element_type=jnp.floa...  56.5 us
    all_gather x1, waiting for transfers between devices, shards(): gathered = lax.all_gather(own_slices, 'code', axis=0, tiled=True)  50.9 us
    dot_general x4, matrix products, advance(): jnp.einsum('rk,rd->kd', weights, block, preferred_element_type=jnp.float32)  37.9 us
  transfers between devices with their start and end apart: 6, of which 6 were waited for; matrix products, arithmetic and copies ran while one was open for 4% of the time, Pallas kernels for 0%

commit v1 on v0

v1 whole, which is shorter than its diff:
```python
import functools

import jax
import jax.numpy as jnp
from jax import lax
from jax.experimental import pallas as pl
from jax.experimental.pallas import tpu as pltpu
from jax.sharding import PartitionSpec as P

MESH = pl.DeviceIdType.MESH
bf16 = jnp.bfloat16
f32 = jnp.float32
momentum = 0.8
half_log2e = 0.5 * 1.4426950408889634
RING = 4
QROWS = 144


def dot(a, b, ca, cb):
    return lax.dot_general(a, b, (((ca,), (cb,)), ((), ())), preferred_element_type=f32)


def gray(s):
    return s + (s // 2) * (1 - 2 * (s % 2))


def kernel(
    heads, tok_ref, cb_ref, cnt_ref, sums_hbm,
    quant_ref, ncnt_ref, ncb_ref, spill,
    e_buf, s_buf, m_buf, c_land, naug, c_t, tsend, x_land, q_acc, stat, stat_land, mloc, f_buf,
    qsend, qland, osend, oland, nsend, nland, ksend, kland,
    e_sem, sums_sem, c_ss, c_rs, h_ss, h_rs, y_ss, y_rs, st_ss, st_rs, q_ss, q_rs, o_ss, o_rs, n_ss, n_rs, k_ss, k_rs,
):
    h = lax.axis_index("head")
    code = lax.axis_index("code")
    y, z = code // RING, code % RING
    width = tok_ref.shape[0]
    codes, hd = cb_ref.shape[1], cb_ref.shape[2]
    tile = x_land.shape[2] // 2

    def at_head(d):
        return (lax.rem(h + d, heads), code)

    def at_y(d):
        return (h, lax.rem(y + d, RING) * RING + z)

    def at_z(d):
        return (h, y * RING + lax.rem(z + d, RING))

    def remote(src, dst, ss, rs, where):
        return pltpu.make_async_remote_copy(
            src_ref=src, dst_ref=dst, send_sem=ss, recv_sem=rs, device_id=where, device_id_type=MESH
        )

    sums_buf = s_buf.at[1, :, pl.ds(0, hd)]

    def sum_copy():
        return pltpu.make_async_copy(sums_hbm.at[0], sums_buf, sums_sem)

    barrier = pltpu.get_barrier_semaphore()
    for d in range(1, heads):
        pl.semaphore_signal(barrier, inc=1, device_id=at_head(d), device_id_type=MESH)
    for d in range(1, RING):
        pl.semaphore_signal(barrier, inc=1, device_id=at_y(d), device_id_type=MESH)
        pl.semaphore_signal(barrier, inc=1, device_id=at_z(d), device_id_type=MESH)
    for g in range(heads):
        block = tok_ref[:, g * hd:(g + 1) * hd].astype(f32)
        tsend[g] = jnp.transpose(block).astype(bf16)
    pl.semaphore_wait(barrier, heads - 1 + 2 * (RING - 1))

    def head_copy(d):
        return remote(
            tsend.at[lax.rem(h + d, heads)],
            x_land.at[y, :, pl.ds(pl.multiple_of(h * width, 128), width)],
            h_ss.at[d - 1], h_rs.at[d - 1], at_head(d),
        )

    def c_copy(d):
        return remote(cb_ref.at[0], c_land.at[z], c_ss.at[d - 1], c_rs.at[d - 1], at_z(d))

    def y_copy(d):
        return remote(x_land.at[y], x_land.at[y], y_ss.at[d - 1], y_rs.at[d - 1], at_y(d))

    for d in range(1, heads):
        head_copy(d).start()
    for d in (1, 3, 2):
        c_copy(d).start()
    x_land[y, :, pl.ds(pl.multiple_of(h * width, 128), width)] = tsend[h]
    c_land[z] = cb_ref[0]

    for slot in range(2):
        lane = lax.broadcasted_iota(jnp.int32, (QROWS - hd, codes), 0)
        c_t[slot, hd:, :] = jnp.where(lane == 0, 1.0, 0.0).astype(bf16)
    row = lax.broadcasted_iota(jnp.int32, (hd, tile), 0)
    ones_rows = jnp.where(row < 3, 1.0, 0.0).astype(bf16)

    def prepare(slot, zb):
        c = c_land[zb].astype(f32)
        n = -0.5 * jnp.sum(c * c, axis=1, keepdims=True)
        hi = n.astype(bf16).astype(f32)
        rest = n - hi
        mid = rest.astype(bf16).astype(f32)
        low = rest - mid
        lane = lax.broadcasted_iota(jnp.int32, (codes, hd), 1)
        naug[slot] = jnp.where(lane == 0, hi, jnp.where(lane == 1, mid, jnp.where(lane == 2, low, 0.0))).astype(bf16)
        c_t[slot, 0:hd, :] = jnp.transpose(c).astype(bf16)

    prepare(0, z)
    stat[0] = jnp.full(stat.shape[1:], -3e38, f32)
    q_acc[...] = jnp.zeros(q_acc.shape, f32)

    for d in range(1, heads):
        head_copy(d).wait()
    for d in (1, 3, 2):
        y_copy(d).start()

    def logits(j, s, half, slot):
        zb = lax.rem(z + gray(j), RING)
        yb = lax.rem(y + gray(s), RING)
        left = jnp.concatenate([c_land[zb], naug[j % 2]], axis=1)
        right = jnp.concatenate([x_land[yb, :, half * tile:(half + 1) * tile], ones_rows], axis=0)
        out = dot(left, right, 1, 0)
        s_buf[slot] = out
        m_buf[slot] = jnp.max(out, axis=0, keepdims=True)

    def finish(j, s, half, slot):
        ta = 2 * lax.rem(y + gray(s), RING) + half
        es = (j % 2) * (2 * RING) + 2 * s + half
        m = m_buf[slot]
        e = jnp.exp2((s_buf[slot] - m) * half_log2e).astype(bf16)
        e_buf[es] = e
        q = dot(c_t[j % 2], e, 1, 0)
        m_old = stat[0, pl.ds(ta, 1), :]
        m_new = jnp.maximum(m_old, m)
        q_acc[ta] = q_acc[ta] * jnp.exp2((m_old - m_new) * half_log2e) + q * jnp.exp2((m - m_new) * half_log2e)
        stat[0, pl.ds(ta, 1), :] = m_new
        mloc[j, pl.ds(ta, 1), :] = m

    def spill_copy(es):
        return pltpu.make_async_copy(e_buf.at[es], spill.at[es], e_sem.at[es])

    def fetch_copy(es):
        return pltpu.make_async_copy(spill.at[es], e_buf.at[es], e_sem.at[es])

    pairs = RING * RING
    logits(0, 0, 0, 0)

    def step(p, _):
        j, s = p // RING, p % RING
        pn = (p + 1) % pairs
        jn, sn = pn // RING, pn % RING
        es = (j % 2) * (2 * RING) + 2 * s

        @pl.when(p < RING - 1)
        def _():
            o = gray(p + 1)
            src = lax.rem(y + o, RING)
            remote(x_land.at[src], x_land.at[src], y_ss.at[3 - o], y_rs.at[3 - o], at_y(4 - o)).wait_recv()

        @pl.when((s == RING - 1) & (j < RING - 1))
        def _():
            o = gray(j + 1)
            src = lax.rem(z + o, RING)
            remote(cb_ref.at[0], c_land.at[src], c_ss.at[3 - o], c_rs.at[3 - o], at_z(4 - o)).wait_recv()
            prepare(jn % 2, src)

        @pl.when(j >= 2)
        def _():
            spill_copy(es).wait()
            spill_copy(es + 1).wait()

        logits(j, s, 1, 1)
        finish(j, s, 0, 0)
        logits(jn, sn, 0, 0)
        finish(j, s, 1, 1)

        @pl.when(j < 2)
        def _():
            spill_copy(es).start()
            spill_copy(es + 1).start()

        return 0

    lax.fori_loop(0, pairs, step, 0)
    sum_copy().start()

    for t in range(2 * RING):
        stat[1, t:t + 1, :] = q_acc[t, hd:hd + 1, :]

    def stat_copy(d):
        return remote(stat, stat_land.at[d - 1], st_ss.at[d - 1], st_rs.at[d - 1], at_y(d))

    for d in range(1, RING):
        stat_copy(d).start()
    for d in range(1, RING):
        stat_copy(d).wait()
    top = stat[0]
    for d in range(1, RING):
        top = jnp.maximum(top, stat_land[d - 1, 0])
    total = stat[1] * jnp.exp2((stat[0] - top) * half_log2e)
    for d in range(1, RING):
        total = total + stat_land[d - 1, 1] * jnp.exp2((stat_land[d - 1, 0] - top) * half_log2e)
    inverse = 1.0 / total
    for j in range(RING):
        f_buf[j] = jnp.exp2((mloc[j] - top) * half_log2e) * inverse
    gain = jnp.exp2((stat[0] - top) * half_log2e) * inverse
    for t in range(2 * RING):
        qsend[t // 2, :, (t % 2) * tile:(t % 2 + 1) * tile] = (q_acc[t, 0:hd, :] * gain[t:t + 1, :]).astype(bf16)

    def q_copy(d):
        return remote(
            qsend.at[lax.rem(y + d, RING)], qland.at[d - 1], q_ss.at[d - 1], q_rs.at[d - 1], at_y(d)
        )

    for d in (2, 1, 3):
        q_copy(d).start()

    def o_copy(d):
        return remote(osend.at[lax.rem(h + d, heads)], oland.at[h], o_ss.at[d - 1], o_rs.at[d - 1], at_head(d))

    def send_quantized():
        for d in range(1, RING):
            q_copy(d).wait()
        for g in range(heads):
            cols = slice(g * width, (g + 1) * width)
            block = qsend[y, :, cols].astype(f32)
            for d in range(1, RING):
                block = block + qland[d - 1, :, cols].astype(f32)
            osend[g] = jnp.transpose(block).astype(bf16)
        for d in range(1, heads):
            o_copy(d).start()
        oland[h] = osend[h]

    group = 4
    acc = s_buf.at[0]
    pad_row = lax.broadcasted_iota(jnp.int32, (hd, tile), 0)

    def n_copy(jj, d):
        return remote(nsend.at[jj], nland.at[d - 1], n_ss.at[d - 1], n_rs.at[d - 1], at_z(d))

    def k_copy(jj, d):
        return remote(ksend.at[jj], kland.at[d - 1], k_ss.at[d - 1], k_rs.at[d - 1], at_z(d))

    count_row = None
    for jj in range(RING):
        j = RING - 1 - jj
        base = (j % 2) * (2 * RING)

        def partial_sums(g, _, j=j, jj=jj, base=base):
            lefts, rights = [], []
            if jj >= 2:
                for u in range(group):
                    fetch_copy(base + group * g + u).wait()
            for u in range(group):
                s = (group // 2) * g + u // 2
                yb = lax.rem(y + gray(s), RING)
                ta = 2 * yb + u % 2
                f = f_buf[j, pl.ds(ta, 1), :]
                x = x_land[yb, :, (u % 2) * tile:(u % 2 + 1) * tile].astype(f32)
                f_hi = f.astype(bf16).astype(f32)
                extra = jnp.where(pad_row == 0, f_hi, jnp.where(pad_row == 1, f - f_hi, 0.0))
                rights.append(jnp.concatenate([(x * f).astype(bf16), extra.astype(bf16)], axis=0))
                lefts.append(e_buf[base + group * g + u])
            part = dot(jnp.concatenate(lefts, axis=1), jnp.concatenate(rights, axis=1), 1, 1)
            acc[:, 0:2 * hd] = acc[:, 0:2 * hd] + part
            if jj < 2:
                for u in range(group):
                    fetch_copy(base + group * g + u).start()
            return 0

        acc[:, 0:2 * hd] = jnp.zeros((codes, 2 * hd), f32)
        lax.fori_loop(0, 2 * RING // group, partial_sums, 0)
        counts = jnp.transpose(acc[:, hd:2 * hd])
        count_row = counts[0:1, :] + counts[1:2, :]
        if j > 0:
            d = (2, 3, 1)[jj]
            nsend[jj] = acc[:, 0:hd].astype(bf16)
            ksend[jj] = jnp.broadcast_to(count_row, ksend.shape[1:])
            n_copy(jj, d).start()
            k_copy(jj, d).start()
        if jj == 0:
            send_quantized()

    for jj, d in enumerate((2, 3, 1)):
        n_copy(jj, d).wait()
        k_copy(jj, d).wait()
    sum_copy().wait()
    for d in range(1, RING):
        count_row = count_row + kland[d - 1, 0:1, :]
    new_counts = momentum * cnt_ref[...] + (1.0 - momentum) * count_row
    ncnt_ref[...] = new_counts
    inverse_counts = jnp.transpose(jnp.broadcast_to(1.0 / new_counts, (8, codes)))[:, 0:1]
    numerators = acc[:, 0:hd]
    for d in range(1, RING):
        numerators = numerators + nland[d - 1].astype(f32)
    ncb_ref[0] = (momentum * sums_buf[...] + (1.0 - momentum) * numerators) * inverse_counts

    for d in range(1, heads):
        o_copy(d).wait()
    for g in range(heads):
        quant_ref[:, g * hd:(g + 1) * hd] = oland[g]
    for d in (1, 3, 2):
        c_copy(d).wait_send()
        y_copy(d).wait_send()


def shards(tokens, codebook, ema_counts, ema_sums):
    heads = lax.axis_size("head")
    width, _ = tokens.shape
    _, codes, hd = codebook.shape
    rows = heads * width
    tile = rows // 2
    vmem = pl.BlockSpec(memory_space=pltpu.VMEM)
    dma = pltpu.SemaphoreType.DMA
    anywhere = pl.BlockSpec(memory_space=pl.ANY)
    far = RING - 1
    quantized, counts, book, _ = pl.pallas_call(
        functools.partial(kernel, heads),
        out_shape=(
            jax.ShapeDtypeStruct(tokens.shape, bf16),
            jax.ShapeDtypeStruct(ema_counts.shape, f32),
            jax.ShapeDtypeStruct(ema_sums.shape, f32),
            jax.ShapeDtypeStruct((4 * RING, codes, tile), bf16),
        ),
        in_specs=[vmem, vmem, vmem, anywhere],
        out_specs=(vmem, vmem, vmem, anywhere),
        scratch_shapes=[
            pltpu.VMEM((4 * RING, codes, tile), bf16),
            pltpu.VMEM((2, codes, tile), f32),
            pltpu.VMEM((2, 1, tile), f32),
            pltpu.VMEM((RING, codes, hd), bf16),
            pltpu.VMEM((2, codes, hd), bf16),
            pltpu.VMEM((2, QROWS, codes), bf16),
            pltpu.VMEM((heads, hd, width), bf16),
            pltpu.VMEM((RING, hd, rows), bf16),
            pltpu.VMEM((2 * RING, QROWS, tile), f32),
            pltpu.VMEM((2, 2 * RING, tile), f32),
            pltpu.VMEM((far, 2, 2 * RING, tile), f32),
            pltpu.VMEM((RING, 2 * RING, tile), f32),
            pltpu.VMEM((RING, 2 * RING, tile), f32),
            pltpu.VMEM((RING, hd, rows), bf16),
            pltpu.VMEM((far, hd, rows), bf16),
            pltpu.VMEM((heads, width, hd), bf16),
            pltpu.VMEM((heads, width, hd), bf16),
            pltpu.VMEM((far, codes, hd), bf16),
            pltpu.VMEM((far, codes, hd), bf16),
            pltpu.VMEM((far, 8, codes), f32),
            pltpu.VMEM((far, 8, codes), f32),
            dma((4 * RING,)),
            dma,
            dma((far,)), dma((far,)),
            dma((max(heads - 1, 1),)), dma((max(heads - 1, 1),)),
            dma((far,)), dma((far,)),
            dma((far,)), dma((far,)),
            dma((far,)), dma((far,)),
            dma((max(heads - 1, 1),)), dma((max(heads - 1, 1),)),
            dma((far,)), dma((far,)),
            dma((far,)), dma((far,)),
        ],
        compiler_params=pltpu.CompilerParams(
            collective_id=0, has_side_effects=True, vmem_limit_bytes=63 * 2**20
        ),
    )(tokens, codebook, ema_counts, ema_sums)
    return quantized, counts, book


def solution(mesh):
    placed = (
        P(("head", "code"), None),
        P("head", "code", None),
        P("head", "code"),
        P("head", "code", None),
    )
    return jax.shard_map(
        shards,
        mesh=mesh,
        in_specs=placed,
        out_specs=(P(("head", "code"), None), P("head", "code"), P("head", "code", None)),
        check_vma=False,
    )
```

time: 1180 us -> 114 us (0.10)
  blocking collectives: 579 us -> 0 us
  waiting for transfers between devices: 296 us -> 0 us
  other arithmetic: 131 us -> 0 us
  matrix products: 118 us -> 0 us
  Pallas kernels: 0 us -> 106 us
  local copies, waits for them, and re-layouts: 37.1 us -> 5.23 us
  between operations: 13.8 us -> 0.64 us
    pmax x4 -> x0, blocking collectives: 289 us -> none  [advance(): row_peak = lax.pmax(jnp.max(logits, axis=1), 'code')]
    psum x4 -> x0, blocking collectives: 279 us -> none  [advance(): row_sums = lax.psum(jnp.sum(exponent, axis=1), 'code')]
    reduce_scatter x4 -> x0, waiting for transfers between devices: 240 us -> none  [advance(): lax.psum_scatter(partial_rows.astype(jnp.bfloat16), 'code', scatter_dimen...]
    reduce_sum x9 -> x0, other arithmetic: 129 us -> none  [the longest x4 67.9 us: advance(): assigned = assigned + jnp.sum(softmax_out, axis=0)]
    dot_general x12 -> x0, matrix products: 118 us -> none  [the longest x4 56.5 us: advance(): jnp.einsum('rd,kd->rk', block, centroids, preferred_element_type=jnp.floa...]
    pallas_call x0 -> x1, Pallas kernels: none -> 106 us  [shards(): pl.pallas_call(functools.partial(kernel, heads), out_shape=(jax.ShapeDtyp...]
    all_gather x1 -> x0, waiting for transfers between devices: 50.9 us -> none  [shards(): gathered = lax.all_gather(own_slices, 'code', axis=0, tiled=True)]
    while x16 -> x0, local copies, waits for them, and re-layouts: 22.8 us -> none
  transfers between devices with their start and end apart: 6 -> 0, of which waited for: 6 -> 0; matrix products, arithmetic and copies ran while one was open for 4% -> 0% of each run, Pallas kernels for 0% -> 0%
where the time goes in v1:
time: 114 us; the launch traced here: 112 us
  Pallas kernels  106 us (93%)
  local copies, waits for them, and re-layouts  5.23 us (5%)
    pallas_call x1, Pallas kernels, shards(): pl.pallas_call(functools.partial(kernel, heads), out_shape=(jax.ShapeDtyp...  106 us
    unnamed x3, local copies, waits for them, and re-layouts  5.23 us

profile of v1, /device:TPU:0, one launch (start us, length us, event | category | flops | bytes accessed | tf_op | source)
XLA Modules:
  0.0 112.3 jit_solution(2057686298531618256)
XLA Ops:
  0.6 106.5 %shard_map.67 = (bf16[128,1024]{1,0:T(8,128)(2,1)}, f32[1,2048]{1,0:T(1,128)}, f32[1,2048,128]{2,1,0:T(8,128)}, bf16[16,2048,512]{2,1,0:T(8,128)(2,1)}) custom-call(bf16[128,1024]{1,0:T(8,128)(2,1)} %tok_ref.1, bf16[1,2048,128]{2,1,0:T(8,128)(2,1)} %cb_ref.1, f32[1,2048]{1,0:T(1,128)} %cnt_ref.1, f32[1,2048,128]{2,1,0:T(8,128)} %sums_hbm.1), custom_call_target="tpu_custom_call" | custom-call | tf_op jit(solution)/shard_map/pallas_call | solution.py:317
  107.1 1.7 %copy.10 = bf16[128,1024]{1,0:T(8,128)(2,1)} copy(bf16[128,1024]{1,0:T(8,128)(2,1)} %get-tuple-element.12) | data formatting | bytes 524288
  108.8 1.3 %copy.11 = f32[1,2048]{1,0:T(1,128)} copy(f32[1,2048]{1,0:T(1,128)} %get-tuple-element.13) | data formatting | bytes 16384
  110.1 2.3 %copy.12 = f32[1,2048,128]{2,1,0:T(8,128)} copy(f32[1,2048,128]{2,1,0:T(8,128)} %get-tuple-element.14) | data formatting | bytes 2097152

commit v2 on v1

v2 whole, which is shorter than its diff:
```python
import functools

import jax
import jax.numpy as jnp
from jax import lax
from jax.experimental import pallas as pl
from jax.experimental.pallas import tpu as pltpu
from jax.sharding import PartitionSpec as P

MESH = pl.DeviceIdType.MESH
bf16 = jnp.bfloat16
f32 = jnp.float32
momentum = 0.8
half_log2e = 0.5 * 1.4426950408889634
RING = 4
QROWS = 144


def dot(a, b, ca, cb):
    return lax.dot_general(a, b, (((ca,), (cb,)), ((), ())), preferred_element_type=f32)


def gray(s):
    return s + (s // 2) * (1 - 2 * (s % 2))


def kernel(
    heads, tok_ref, cb_ref, cnt_ref, sums_hbm,
    oland, ncnt_ref, ncb_hbm, spill,
    e_buf, s_buf, m_buf, c_land, naug, c_t, naug_next, c_t_next, tsend, x_land, q_acc, stat, stat_land, mloc, f_buf,
    qsend, qland, nsend, nland, ksend, kland,
    e_sem, sums_sem, own_sem, book_sem, c_ss, c_rs, h_ss, h_rs, y_ss, y_rs, st_ss, st_rs, q_ss, q_rs, o_ss, o_rs, n_ss, n_rs, k_ss, k_rs,
):
    h = lax.axis_index("head")
    code = lax.axis_index("code")
    y, z = code // RING, code % RING
    width = tok_ref.shape[0]
    codes, hd = cb_ref.shape[1], cb_ref.shape[2]
    tile = x_land.shape[2] // 2

    def at_head(d):
        return (lax.rem(h + d, heads), code)

    def at_y(d):
        return (h, lax.rem(y + d, RING) * RING + z)

    def at_z(d):
        return (h, y * RING + lax.rem(z + d, RING))

    def remote(src, dst, ss, rs, where):
        return pltpu.make_async_remote_copy(
            src_ref=src, dst_ref=dst, send_sem=ss, recv_sem=rs, device_id=where, device_id_type=MESH
        )

    sums_buf = s_buf.at[1, :, pl.ds(0, hd)]

    def sum_copy():
        return pltpu.make_async_copy(sums_hbm.at[0], sums_buf, sums_sem)

    barrier = pltpu.get_barrier_semaphore()
    for d in range(1, heads):
        pl.semaphore_signal(barrier, inc=1, device_id=at_head(d), device_id_type=MESH)
    for d in range(1, RING):
        pl.semaphore_signal(barrier, inc=1, device_id=at_y(d), device_id_type=MESH)
        pl.semaphore_signal(barrier, inc=1, device_id=at_z(d), device_id_type=MESH)
    for g in range(heads):
        block = tok_ref[:, g * hd:(g + 1) * hd].astype(f32)
        tsend[g] = jnp.transpose(block).astype(bf16)
    pl.semaphore_wait(barrier, heads - 1 + 2 * (RING - 1))

    def head_copy(d):
        return remote(
            tsend.at[lax.rem(h + d, heads)],
            x_land.at[y, :, pl.ds(pl.multiple_of(h * width, 128), width)],
            h_ss.at[d - 1], h_rs.at[d - 1], at_head(d),
        )

    def c_copy(d):
        return remote(cb_ref.at[0], c_land.at[z], c_ss.at[d - 1], c_rs.at[d - 1], at_z(d))

    def y_copy(d, half):
        block = x_land.at[y, :, pl.ds(half * tile, tile)]
        return remote(block, block, y_ss.at[half, d - 1], y_rs.at[half, d - 1], at_y(d))

    for d in range(1, heads):
        head_copy(d).start()
    for d in (1, 3):
        c_copy(d).start()
    x_land[y, :, pl.ds(pl.multiple_of(h * width, 128), width)] = tsend[h]
    c_land[z] = cb_ref[0]

    tail = lax.broadcasted_iota(jnp.int32, (QROWS - hd, codes), 0)
    for slot in range(2):
        c_t[slot, hd:, :] = jnp.where(tail == 0, 1.0, 0.0).astype(bf16)
    row = lax.broadcasted_iota(jnp.int32, (hd, tile), 0)
    ones_rows = jnp.where(row < 3, 1.0, 0.0).astype(bf16)

    def prepare(aug, cols, zb, start, count):
        part = pl.ds(start, count)
        c = c_land[zb, part, :].astype(f32)
        n = -0.5 * jnp.sum(c * c, axis=1, keepdims=True)
        hi = n.astype(bf16).astype(f32)
        rest = n - hi
        mid = rest.astype(bf16).astype(f32)
        low = rest - mid
        lane = lax.broadcasted_iota(jnp.int32, (count, hd), 1)
        aug[part, :] = jnp.where(lane == 0, hi, jnp.where(lane == 1, mid, jnp.where(lane == 2, low, 0.0))).astype(bf16)
        cols[0:hd, part] = jnp.transpose(c).astype(bf16)

    prepare(naug.at[0], c_t.at[0], z, 0, codes)
    stat[...] = jnp.full(stat.shape, -3e38, f32)
    q_acc[...] = jnp.zeros(q_acc.shape, f32)

    for d in range(1, heads):
        head_copy(d).wait()
    for half in range(2):
        for d in (1, 3):
            y_copy(d, half).start()

    def row_block(j, s):
        first = 1 - (j + 3) // 4
        return lax.rem(first * (y + gray(s)) + (1 - first) * s, RING)

    def logits(j, s, half, slot):
        zb = lax.rem(z + gray(j), RING)
        yb = row_block(j, s)
        left = jnp.concatenate([c_land[zb], naug[j % 2]], axis=1)
        right = jnp.concatenate([x_land[yb, :, half * tile:(half + 1) * tile], ones_rows], axis=0)
        out = dot(left, right, 1, 0)
        s_buf[slot] = out
        m_buf[slot] = jnp.max(out, axis=0, keepdims=True)

    def finish(j, s, half, slot):
        yb = row_block(j, s)
        es = (j % 2) * (2 * RING) + 2 * s + half
        m = m_buf[slot]
        e = jnp.exp2((s_buf[slot] - m) * half_log2e).astype(bf16)
        e_buf[es] = e
        q = dot(c_t[j % 2], e, 1, 0)
        m_old = stat[yb, half:half + 1, :]
        m_new = jnp.maximum(m_old, m)
        q = q_acc[2 * yb + half] * jnp.exp2((m_old - m_new) * half_log2e) + q * jnp.exp2((m - m_new) * half_log2e)
        q_acc[2 * yb + half] = q
        stat[yb, half:half + 1, :] = m_new
        stat[yb, 2 + half:3 + half, :] = q[hd:hd + 1, :]
        mloc[yb, pl.ds(2 * j + half, 1), :] = m

    def spill_copy(es):
        return pltpu.make_async_copy(e_buf.at[es], spill.at[es], e_sem.at[es])

    def fetch_copy(es):
        return pltpu.make_async_copy(spill.at[es], e_buf.at[es], e_sem.at[es])

    def wait_rows(s, half):
        o = gray(s)
        block = x_land.at[lax.rem(y + o, RING), :, pl.ds(half * tile, tile)]
        remote(block, block, y_ss.at[half, 3 - o], y_rs.at[half, 3 - o], at_y(4 - o)).wait_recv()

    def wait_codes(j):
        o = gray(j)
        remote(
            cb_ref.at[0], c_land.at[lax.rem(z + o, RING)], c_ss.at[3 - o], c_rs.at[3 - o], at_z(4 - o)
        ).wait_recv()

    def jn_of(j):
        return (j + 1) % RING

    def stat_copy(b, d):
        return remote(stat.at[b], stat_land.at[d - 1, b], st_ss.at[b, d - 1], st_rs.at[b, d - 1], at_y(d))

    pairs = RING * RING
    quarter = codes // RING
    logits(0, 0, 0, 0)

    def step(p, _):
        j, s = p // RING, p % RING
        pn = (p + 1) % pairs
        jn, sn = pn // RING, pn % RING
        es = (j % 2) * (2 * RING) + 2 * s

        @pl.when(p < RING - 1)
        def _():
            wait_rows(p + 1, 0)

        @pl.when((p > 0) & (p < RING))
        def _():
            wait_rows(p, 1)

        @pl.when(p == 1)
        def _():
            for half in range(2):
                for d in (1, 3):
                    y_copy(d, half).wait_send()
            for half in range(2):
                y_copy(2, half).start()

        @pl.when(p == 3)
        def _():
            for d in (1, 3):
                c_copy(d).wait_send()
            c_copy(2).start()
            wait_codes(1)
            prepare(naug.at[1], c_t.at[1], lax.rem(z + 1, RING), 0, codes)

        @pl.when((s == 0) & (j > 0) & (j < RING - 1))
        def _():
            wait_codes(j + 1)

        ahead = lax.rem(z + gray(jn_of(j)) * ((j + 3) // 4), RING)

        @pl.when((s == RING - 1) & (j > 0) & (j < RING - 1))
        def _():
            slot = jn_of(j) % 2
            done = (RING - 1) * quarter
            naug[slot, 0:done, :] = naug_next[0:done, :]
            c_t[slot, 0:hd, 0:done] = c_t_next[0:hd, 0:done]
            prepare(naug.at[slot], c_t.at[slot], ahead, done, quarter)

        @pl.when(j >= 2)
        def _():
            spill_copy(es).wait()
            spill_copy(es + 1).wait()

        logits(j, s, 1, 1)
        finish(j, s, 0, 0)
        logits(jn, sn, 0, 0)
        finish(j, s, 1, 1)
        prepare(naug_next, c_t_next, ahead, pl.multiple_of(s * quarter, quarter), quarter)

        @pl.when(j == RING - 1)
        def _():
            for d in range(1, RING):
                stat_copy(s, d).start()

        @pl.when(j < 2)
        def _():
            spill_copy(es).start()
            spill_copy(es + 1).start()

        return 0

    lax.fori_loop(0, pairs, step, 0)
    sum_copy().start()

    def q_copy(b):
        d = lax.rem(b - y + RING, RING)
        return remote(qsend.at[b], qland.at[d - 1], q_ss.at[d - 1], q_rs.at[d - 1], (h, b * RING + z))

    def q_wait(d):
        b = lax.rem(y + d, RING)
        return remote(qsend.at[b], qland.at[d - 1], q_ss.at[d - 1], q_rs.at[d - 1], (h, b * RING + z))

    def totals(b):
        for d in range(1, RING):
            stat_copy(b, d).wait()
        m, l = stat[b, 0:2, :], stat[b, 2:4, :]
        top = m
        for d in range(1, RING):
            top = jnp.maximum(top, stat_land[d - 1, b, 0:2, :])
        total = l * jnp.exp2((m - top) * half_log2e)
        for d in range(1, RING):
            total = total + stat_land[d - 1, b, 2:4, :] * jnp.exp2((stat_land[d - 1, b, 0:2, :] - top) * half_log2e)
        inverse = 1.0 / total
        gain = jnp.exp2((m - top) * half_log2e) * inverse
        even = lax.broadcasted_iota(jnp.int32, (2 * RING, tile), 0) % 2 == 0
        top_all = jnp.where(even, top[0:1, :], top[1:2, :])
        f_buf[b] = jnp.exp2((mloc[b] - top_all) * half_log2e) * jnp.where(even, inverse[0:1, :], inverse[1:2, :])
        for half in range(2):
            cols = slice(half * tile, (half + 1) * tile)
            qsend[b, :, cols] = (q_acc[2 * b + half, 0:hd, :] * gain[half:half + 1, :]).astype(bf16)

        @pl.when(y != b)
        def _():
            q_copy(b).start()

    def o_copy(d):
        return remote(tsend.at[lax.rem(h + d, heads)], oland.at[h], o_ss.at[d - 1], o_rs.at[d - 1], at_head(d))

    def send_quantized():
        for d in range(1, RING):
            q_wait(d).wait()
        for g in range(heads):
            cols = slice(g * width, (g + 1) * width)
            block = qsend[y, :, cols].astype(f32)
            for d in range(1, RING):
                block = block + qland[d - 1, :, cols].astype(f32)
            tsend[g] = jnp.transpose(block).astype(bf16)
        for d in range(1, heads):
            o_copy(d).start()
        pltpu.make_async_copy(tsend.at[h], oland.at[h], own_sem).start()

    group = 4
    half_codes = codes // 2
    acc = s_buf.at[0, :, pl.ds(0, 2 * hd)]
    pad_row = lax.broadcasted_iota(jnp.int32, (hd, tile), 0)

    def n_copy(jj, d, ch):
        part = pl.ds(pl.multiple_of(ch * half_codes, half_codes), half_codes)
        return remote(nsend.at[jj, part], nland.at[d - 1, part], n_ss.at[d - 1, ch], n_rs.at[d - 1, ch], at_z(d))

    def k_copy(jj, d, ch):
        part = pl.ds(pl.multiple_of(ch * half_codes, half_codes), half_codes)
        return remote(
            ksend.at[jj, :, part], kland.at[d - 1, :, part], k_ss.at[d - 1, ch], k_rs.at[d - 1, ch], at_z(d)
        )

    def scaled(j, t):
        yb = row_block(j, t // 2)
        f = f_buf[yb, 2 * j + t % 2:2 * j + t % 2 + 1, :]
        x = x_land[yb, :, (t % 2) * tile:(t % 2 + 1) * tile].astype(f32)
        f_hi = f.astype(bf16).astype(f32)
        extra = jnp.where(pad_row == 0, f_hi, jnp.where(pad_row == 1, f - f_hi, 0.0))
        return jnp.concatenate([(x * f).astype(bf16), extra.astype(bf16)], axis=0)

    routes = (2, 3, 1)
    for jj in range(RING):
        j = RING - 1 - jj
        base = (j % 2) * (2 * RING)
        for g in range(2 * RING // group):
            tiles = range(g * group, (g + 1) * group)
            if jj == 0:
                for b in range(g * group // 2, (g + 1) * group // 2):
                    totals(b)
            if jj >= 2:
                for t in tiles:
                    fetch_copy(base + t).wait()

            def some_codes(ch, _, j=j, jj=jj, base=base, tiles=tiles, g=g):
                part = pl.ds(pl.multiple_of(ch * half_codes, half_codes), half_codes)
                left = jnp.concatenate([e_buf[base + t, part, :] for t in tiles], axis=1)
                right = jnp.concatenate([scaled(j, t) for t in tiles], axis=1)
                out = dot(left, right, 1, 1)
                if g > 0:
                    out = out + acc[part, :]
                if g < 2 * RING // group - 1:
                    acc[part, :] = out
                else:
                    columns = jnp.transpose(out[:, hd:2 * hd])
                    row = columns[0:1, :] + columns[1:2, :]
                    ksend[jj, :, part] = jnp.broadcast_to(row, (8, half_codes))
                    if j > 0:
                        nsend[jj, part, :] = out[:, 0:hd].astype(bf16)
                        n_copy(jj, routes[jj], ch).start()
                        k_copy(jj, routes[jj], ch).start()
                    else:
                        acc[part, 0:hd] = out[:, 0:hd]
                return 0

            lax.fori_loop(0, 2, some_codes, 0)
            if jj < 2:
                for t in tiles:
                    fetch_copy(base + t).start()
        if jj == 2:
            send_quantized()

    sum_copy().wait()
    book_copies = []
    for ch in range(2):
        part = slice(ch * half_codes, (ch + 1) * half_codes)
        for jj, d in enumerate(routes):
            n_copy(jj, d, ch).wait()
            k_copy(jj, d, ch).wait()
        row = ksend[RING - 1, 0:1, part]
        numerators = acc[part, 0:hd]
        for d in range(1, RING):
            row = row + kland[d - 1, 0:1, part]
            numerators = numerators + nland[d - 1, part, :].astype(f32)
        new_counts = momentum * cnt_ref[:, part] + (1.0 - momentum) * row
        ncnt_ref[:, part] = new_counts
        inverse_counts = jnp.transpose(jnp.broadcast_to(1.0 / new_counts, (8, half_codes)))[:, 0:1]
        sums_buf[part, :] = (momentum * sums_buf[part, :] + (1.0 - momentum) * numerators) * inverse_counts
        book_copies.append(
            pltpu.make_async_copy(
                sums_buf.at[pl.ds(ch * half_codes, half_codes)],
                ncb_hbm.at[0, pl.ds(ch * half_codes, half_codes)],
                book_sem.at[ch],
            )
        )
        book_copies[-1].start()
    for d in range(1, heads):
        o_copy(d).wait()
    pltpu.make_async_copy(tsend.at[h], oland.at[h], own_sem).wait()
    c_copy(2).wait_send()
    for half in range(2):
        y_copy(2, half).wait_send()
    for copy in book_copies:
        copy.wait()


def place(oland, counts, book, quant_ref, ncnt_ref, ncb_ref):
    heads, _, hd = oland.shape
    for g in range(heads):
        quant_ref[:, g * hd:(g + 1) * hd] = oland[g]
    ncnt_ref[...] = counts[...]
    ncb_ref[...] = book[...]


def shards(tokens, codebook, ema_counts, ema_sums):
    heads = lax.axis_size("head")
    width, _ = tokens.shape
    _, codes, hd = codebook.shape
    rows = heads * width
    tile = rows // 2
    vmem = pl.BlockSpec(memory_space=pltpu.VMEM)
    dma = pltpu.SemaphoreType.DMA
    anywhere = pl.BlockSpec(memory_space=pl.ANY)
    far = RING - 1
    pieces, counts, book, _ = pl.pallas_call(
        functools.partial(kernel, heads),
        out_shape=(
            jax.ShapeDtypeStruct((heads, width, hd), bf16),
            jax.ShapeDtypeStruct(ema_counts.shape, f32),
            jax.ShapeDtypeStruct(ema_sums.shape, f32),
            jax.ShapeDtypeStruct((4 * RING, codes, tile), bf16),
        ),
        in_specs=[vmem, vmem, vmem, anywhere],
        out_specs=(anywhere, vmem, anywhere, anywhere),
        scratch_shapes=[
            pltpu.VMEM((4 * RING, codes, tile), bf16),
            pltpu.VMEM((2, codes, tile), f32),
            pltpu.VMEM((2, 1, tile), f32),
            pltpu.VMEM((RING, codes, hd), bf16),
            pltpu.VMEM((2, codes, hd), bf16),
            pltpu.VMEM((2, QROWS, codes), bf16),
            pltpu.VMEM((codes, hd), bf16),
            pltpu.VMEM((hd, codes), bf16),
            pltpu.VMEM((heads, hd, width), bf16),
            pltpu.VMEM((RING, hd, rows), bf16),
            pltpu.VMEM((2 * RING, QROWS, tile), f32),
            pltpu.VMEM((RING, 8, tile), f32),
            pltpu.VMEM((far, RING, 8, tile), f32),
            pltpu.VMEM((RING, 2 * RING, tile), f32),
            pltpu.VMEM((RING, 2 * RING, tile), f32),
            pltpu.VMEM((RING, hd, rows), bf16),
            pltpu.VMEM((far, hd, rows), bf16),
            pltpu.VMEM((far, codes, hd), bf16),
            pltpu.VMEM((far, codes, hd), bf16),
            pltpu.VMEM((RING, 8, codes), f32),
            pltpu.VMEM((far, 8, codes), f32),
            dma((4 * RING,)),
            dma,
            dma,
            dma((2,)),
            dma((far,)), dma((far,)),
            dma((max(heads - 1, 1),)), dma((max(heads - 1, 1),)),
            dma((2, far)), dma((2, far)),
            dma((RING, far)), dma((RING, far)),
            dma((far,)), dma((far,)),
            dma((max(heads - 1, 1),)), dma((max(heads - 1, 1),)),
            dma((far, 2)), dma((far, 2)),
            dma((far, 2)), dma((far, 2)),
        ],
        compiler_params=pltpu.CompilerParams(
            collective_id=0, has_side_effects=True, vmem_limit_bytes=63 * 2**20
        ),
    )(tokens, codebook, ema_counts, ema_sums)
    return pl.pallas_call(
        place,
        out_shape=(
            jax.ShapeDtypeStruct(tokens.shape, bf16),
            jax.ShapeDtypeStruct(ema_counts.shape, f32),
            jax.ShapeDtypeStruct(ema_sums.shape, f32),
        ),
        in_specs=[vmem] * 3,
        out_specs=(vmem,) * 3,
    )(pieces, counts, book)


def solution(mesh):
    placed = (
        P(("head", "code"), None),
        P("head", "code", None),
        P("head", "code"),
        P("head", "code", None),
    )
    return jax.shard_map(
        shards,
        mesh=mesh,
        in_specs=placed,
        out_specs=(P(("head", "code"), None), P("head", "code"), P("head", "code", None)),
        check_vma=False,
    )
```

time: 114 us -> 103 us (0.904)
  local copies, waits for them, and re-layouts: 5.23 us -> 0 us
  Pallas kernels: 106 us -> 101 us
    pallas_call x1, Pallas kernels: 106 us -> 99 us  [shards(): pl.pallas_call(functools.partial(kernel, heads), out_shape=(jax.ShapeDtyp...]
    unnamed x3 -> x0, local copies, waits for them, and re-layouts: 5.23 us -> none
    pallas_call x0 -> x1, Pallas kernels: none -> 2.46 us  [shards(): pl.pallas_call(place, out_shape=(jax.ShapeDtypeStruct(tokens.shape, bf16)...]
where the time goes in v2:
time: 103 us; the launch traced here: 102 us
  Pallas kernels  101 us (98%)
    pallas_call x1, Pallas kernels, shards(): pl.pallas_call(functools.partial(kernel, heads), out_shape=(jax.ShapeDtyp...  99 us
    pallas_call x1, Pallas kernels, shards(): pl.pallas_call(place, out_shape=(jax.ShapeDtypeStruct(tokens.shape, bf16)...  2.46 us

profile of v2, /device:TPU:0, one launch (start us, length us, event | category | flops | bytes accessed | tf_op | source)
XLA Modules:
  0.0 102.1 jit_solution(9376649699900929760)
XLA Ops:
  0.6 99.0 %shard_map.67 = (bf16[8,128,128]{2,1,0:T(8,128)(2,1)}, f32[1,2048]{1,0:T(1,128)}, f32[1,2048,128]{2,1,0:T(8,128)}, bf16[16,2048,512]{2,1,0:T(8,128)(2,1)}) custom-call(bf16[128,1024]{1,0:T(8,128)(2,1)} %tok_ref.1, bf16[1,2048,128]{2,1,0:T(8,128)(2,1)} %cb_ref.1, f32[1,2048]{1,0:T(1,128)} %cnt_ref.1, f32[1,2048,128]{2,1,0:T(8,128)} %sums_hbm.1), custom_call_target="tpu_custom_call" | custom-call | tf_op jit(solution)/shard_map/pallas_call | solution.py:408
  99.7 2.5 %shard_map.68 = (bf16[128,1024]{1,0:T(8,128)(2,1)}, f32[1,2048]{1,0:T(1,128)}, f32[1,2048,128]{2,1,0:T(8,128)}) custom-call(bf16[8,128,128]{2,1,0:T(8,128)(2,1)} %get-tuple-element.6.oland, f32[1,2048]{1,0:T(1,128)} %get-tuple-element.7.counts, f32[1,2048,128]{2,1,0:T(8,128)} %get-tuple-element.8.book), custom_call_target="tpu_custom_call" | custom-call | tf_op jit(solution)/shard_map/pallas_call | solution.py:457

commit v3 on v2

--- a/solution.py
+++ b/solution.py
@@ -33,7 +33,11 @@
 ):
     h = lax.axis_index("head")
     code = lax.axis_index("code")
-    y, z = code // RING, code % RING
+    core = lax.rem(h, 2)
+    first, second = code // RING, code % RING
+    y = first * (1 - core) + second * core
+    z = second * (1 - core) + first * core
+    y_step, z_step = RING - (RING - 1) * core, 1 + (RING - 1) * core
     width = tok_ref.shape[0]
     codes, hd = cb_ref.shape[1], cb_ref.shape[2]
     tile = x_land.shape[2] // 2
@@ -42,10 +46,10 @@
         return (lax.rem(h + d, heads), code)
 
     def at_y(d):
-        return (h, lax.rem(y + d, RING) * RING + z)
+        return (h, lax.rem(y + d, RING) * y_step + z * z_step)
 
     def at_z(d):
-        return (h, y * RING + lax.rem(z + d, RING))
+        return (h, y * y_step + lax.rem(z + d, RING) * z_step)
 
     def remote(src, dst, ss, rs, where):
         return pltpu.make_async_remote_copy(
@@ -69,9 +73,11 @@
     pl.semaphore_wait(barrier, heads - 1 + 2 * (RING - 1))
 
     def head_copy(d):
+        other = lax.rem(h + d, 2)
+        block = first * (1 - other) + second * other
         return remote(
             tsend.at[lax.rem(h + d, heads)],
-            x_land.at[y, :, pl.ds(pl.multiple_of(h * width, 128), width)],
+            x_land.at[block, :, pl.ds(pl.multiple_of(h * width, 128), width)],
             h_ss.at[d - 1], h_rs.at[d - 1], at_head(d),
         )
 
@@ -162,15 +168,49 @@
             cb_ref.at[0], c_land.at[lax.rem(z + o, RING)], c_ss.at[3 - o], c_rs.at[3 - o], at_z(4 - o)
         ).wait_recv()
 
-    def jn_of(j):
-        return (j + 1) % RING
-
     def stat_copy(b, d):
         return remote(stat.at[b], stat_land.at[d - 1, b], st_ss.at[b, d - 1], st_rs.at[b, d - 1], at_y(d))
 
     pairs = RING * RING
     quarter = codes // RING
     logits(0, 0, 0, 0)
+
+    def first_step(p, _):
+        @pl.when(p > 0)
+        def _():
+            wait_rows(p, 1)
+
+        @pl.when(p == 1)
+        def _():
+            for half in range(2):
+                for d in (1, 3):
+                    y_copy(d, half).wait_send()
+            for half in range(2):
+                y_copy(2, half).start()
+
+        @pl.when(p == 2)
+        def _():
+            for d in (1, 3):
+                c_copy(d).wait_send()
+            c_copy(2).start()
+
+        logits(0, p, 1, 1)
+        finish(0, p, 0, 0)
+
+        @pl.when(p < RING - 1)
+        def _():
+            wait_rows(p + 1, 0)
+
+        @pl.when(p == RING - 1)
+        def _():
+            wait_codes(1)
+            prepare(naug.at[1], c_t.at[1], lax.rem(z + 1, RING), 0, codes)
+
+        logits((p + 1) // RING, (p + 1) % RING, 0, 0)
+        finish(0, p, 1, 1)
+        spill_copy(2 * p).start()
+        spill_copy(2 * p + 1).start()
+        return 0
 
     def step(p, _):
         j, s = p // RING, p % RING
@@ -178,39 +218,15 @@
         jn, sn = pn // RING, pn % RING
         es = (j % 2) * (2 * RING) + 2 * s
 
-        @pl.when(p < RING - 1)
-        def _():
-            wait_rows(p + 1, 0)
-
-        @pl.when((p > 0) & (p < RING))
-        def _():
-            wait_rows(p, 1)
-
-        @pl.when(p == 1)
-        def _():
-            for half in range(2):
-                for d in (1, 3):
-                    y_copy(d, half).wait_send()
-            for half in range(2):
-                y_copy(2, half).start()
-
-        @pl.when(p == 3)
-        def _():
-            for d in (1, 3):
-                c_copy(d).wait_send()
-            c_copy(2).start()
-            wait_codes(1)
-            prepare(naug.at[1], c_t.at[1], lax.rem(z + 1, RING), 0, codes)
-
-        @pl.when((s == 0) & (j > 0) & (j < RING - 1))
+        @pl.when((s == 0) & (j < RING - 1))
         def _():
             wait_codes(j + 1)
 
-        ahead = lax.rem(z + gray(jn_of(j)) * ((j + 3) // 4), RING)
-
-        @pl.when((s == RING - 1) & (j > 0) & (j < RING - 1))
-        def _():
-            slot = jn_of(j) % 2
+        ahead = lax.rem(z + gray((j + 1) % RING), RING)
+
+        @pl.when((s == RING - 1) & (j < RING - 1))
+        def _():
+            slot = (j + 1) % 2
             done = (RING - 1) * quarter
             naug[slot, 0:done, :] = naug_next[0:done, :]
             c_t[slot, 0:hd, 0:done] = c_t_next[0:hd, 0:done]
@@ -239,16 +255,17 @@
 
         return 0
 
-    lax.fori_loop(0, pairs, step, 0)
+    lax.fori_loop(0, RING, first_step, 0)
+    lax.fori_loop(RING, pairs, step, 0)
     sum_copy().start()
 
     def q_copy(b):
         d = lax.rem(b - y + RING, RING)
-        return remote(qsend.at[b], qland.at[d - 1], q_ss.at[d - 1], q_rs.at[d - 1], (h, b * RING + z))
+        return remote(qsend.at[b], qland.at[d - 1], q_ss.at[d - 1], q_rs.at[d - 1], (h, b * y_step + z * z_step))
 
     def q_wait(d):
         b = lax.rem(y + d, RING)
-        return remote(qsend.at[b], qland.at[d - 1], q_ss.at[d - 1], q_rs.at[d - 1], (h, b * RING + z))
+        return remote(qsend.at[b], qland.at[d - 1], q_ss.at[d - 1], q_rs.at[d - 1], (h, b * y_step + z * z_step))
 
     def totals(b):
         for d in range(1, RING):
@@ -337,7 +354,7 @@
                 else:
                     columns = jnp.transpose(out[:, hd:2 * hd])
                     row = columns[0:1, :] + columns[1:2, :]
-                    ksend[jj, :, part] = jnp.broadcast_to(row, (8, half_codes))
+                    ksend[jj, :, part] = row
                     if j > 0:
                         nsend[jj, part, :] = out[:, 0:hd].astype(bf16)
                         n_copy(jj, routes[jj], ch).start()
@@ -360,10 +377,10 @@
         for jj, d in enumerate(routes):
             n_copy(jj, d, ch).wait()
             k_copy(jj, d, ch).wait()
-        row = ksend[RING - 1, 0:1, part]
+        row = ksend[RING - 1, :, part]
         numerators = acc[part, 0:hd]
         for d in range(1, RING):
-            row = row + kland[d - 1, 0:1, part]
+            row = row + kland[d - 1, :, part]
             numerators = numerators + nland[d - 1, part, :].astype(f32)
         new_counts = momentum * cnt_ref[:, part] + (1.0 - momentum) * row
         ncnt_ref[:, part] = new_counts
@@ -435,8 +452,8 @@
             pltpu.VMEM((far, hd, rows), bf16),
             pltpu.VMEM((far, codes, hd), bf16),
             pltpu.VMEM((far, codes, hd), bf16),
-            pltpu.VMEM((RING, 8, codes), f32),
-            pltpu.VMEM((far, 8, codes), f32),
+            pltpu.VMEM((RING, 1, codes), f32),
+            pltpu.VMEM((far, 1, codes), f32),
             dma((4 * RING,)),
             dma,
             dma,

time: 103 us -> 93 us (0.903)
  Pallas kernels: 101 us -> 92.2 us
    pallas_call x1, Pallas kernels: 99 us -> 89.8 us  [shards(): pl.pallas_call(functools.partial(kernel, heads), out_shape=(jax.ShapeDtyp...]
where the time goes in v3:
time: 93 us; the launch traced here: 92.9 us
  Pallas kernels  92.2 us (99%)
    pallas_call x1, Pallas kernels, shards(): pl.pallas_call(functools.partial(kernel, heads), out_shape=(jax.ShapeDtyp...  89.8 us
    pallas_call x1, Pallas kernels, shards(): pl.pallas_call(place, out_shape=(jax.ShapeDtypeStruct(tokens.shape, bf16)...  2.46 us

profile of v3, /device:TPU:0, one launch (start us, length us, event | category | flops | bytes accessed | tf_op | source)
XLA Modules:
  0.0 92.9 jit_solution(16788382640487102333)
XLA Ops:
  0.6 89.8 %shard_map.67 = (bf16[8,128,128]{2,1,0:T(8,128)(2,1)}, f32[1,2048]{1,0:T(1,128)}, f32[1,2048,128]{2,1,0:T(8,128)}, bf16[16,2048,512]{2,1,0:T(8,128)(2,1)}) custom-call(bf16[128,1024]{1,0:T(8,128)(2,1)} %tok_ref.1, bf16[1,2048,128]{2,1,0:T(8,128)(2,1)} %cb_ref.1, f32[1,2048]{1,0:T(1,128)} %cnt_ref.1, f32[1,2048,128]{2,1,0:T(8,128)} %sums_hbm.1), custom_call_target="tpu_custom_call" | custom-call | tf_op jit(solution)/shard_map/pallas_call | solution.py:425
  90.4 2.5 %shard_map.68 = (bf16[128,1024]{1,0:T(8,128)(2,1)}, f32[1,2048]{1,0:T(1,128)}, f32[1,2048,128]{2,1,0:T(8,128)}) custom-call(bf16[8,128,128]{2,1,0:T(8,128)(2,1)} %get-tuple-element.6.oland, f32[1,2048]{1,0:T(1,128)} %get-tuple-element.7.counts, f32[1,2048,128]{2,1,0:T(8,128)} %get-tuple-element.8.book), custom_call_target="tpu_custom_call" | custom-call | tf_op jit(solution)/shard_map/pallas_call | solution.py:474

commit v4 on v3

--- a/solution.py
+++ b/solution.py
@@ -25,11 +25,11 @@
 
 
 def kernel(
-    heads, tok_ref, cb_ref, cnt_ref, sums_hbm,
+    heads, tok_hbm, cb_hbm, cnt_ref, sums_hbm,
     oland, ncnt_ref, ncb_hbm, spill,
-    e_buf, s_buf, m_buf, c_land, naug, c_t, naug_next, c_t_next, tsend, x_land, q_acc, stat, stat_land, mloc, f_buf,
+    e_buf, s_buf, m_buf, c_land, naug, c_t, naug_next, c_t_next, tok_ref, tsend, x_land, q_acc, stat, stat_land, mloc, f_buf, gain,
     qsend, qland, nsend, nland, ksend, kland,
-    e_sem, sums_sem, own_sem, book_sem, c_ss, c_rs, h_ss, h_rs, y_ss, y_rs, st_ss, st_rs, q_ss, q_rs, o_ss, o_rs, n_ss, n_rs, k_ss, k_rs,
+    e_sem, sums_sem, own_sem, book_sem, in_sem, c_ss, c_rs, h_ss, h_rs, y_ss, y_rs, st_ss, st_rs, q_ss, q_rs, o_ss, o_rs, n_ss, n_rs, k_ss, k_rs,
 ):
     h = lax.axis_index("head")
     code = lax.axis_index("code")
@@ -39,7 +39,7 @@
     z = second * (1 - core) + first * core
     y_step, z_step = RING - (RING - 1) * core, 1 + (RING - 1) * core
     width = tok_ref.shape[0]
-    codes, hd = cb_ref.shape[1], cb_ref.shape[2]
+    codes, hd = cb_hbm.shape[1], cb_hbm.shape[2]
     tile = x_land.shape[2] // 2
 
     def at_head(d):
@@ -60,6 +60,11 @@
 
     def sum_copy():
         return pltpu.make_async_copy(sums_hbm.at[0], sums_buf, sums_sem)
+
+    tok_copy = pltpu.make_async_copy(tok_hbm, tok_ref, in_sem.at[0])
+    tok_copy.start()
+    own_codes = pltpu.make_async_copy(cb_hbm.at[0], c_land.at[z], in_sem.at[1])
+    own_codes.start()
 
     barrier = pltpu.get_barrier_semaphore()
     for d in range(1, heads):
@@ -67,6 +72,7 @@
     for d in range(1, RING):
         pl.semaphore_signal(barrier, inc=1, device_id=at_y(d), device_id_type=MESH)
         pl.semaphore_signal(barrier, inc=1, device_id=at_z(d), device_id_type=MESH)
+    tok_copy.wait()
     for g in range(heads):
         block = tok_ref[:, g * hd:(g + 1) * hd].astype(f32)
         tsend[g] = jnp.transpose(block).astype(bf16)
@@ -82,7 +88,7 @@
         )
 
     def c_copy(d):
-        return remote(cb_ref.at[0], c_land.at[z], c_ss.at[d - 1], c_rs.at[d - 1], at_z(d))
+        return remote(cb_hbm.at[0], c_land.at[z], c_ss.at[d - 1], c_rs.at[d - 1], at_z(d))
 
     def y_copy(d, half):
         block = x_land.at[y, :, pl.ds(half * tile, tile)]
@@ -93,7 +99,6 @@
     for d in (1, 3):
         c_copy(d).start()
     x_land[y, :, pl.ds(pl.multiple_of(h * width, 128), width)] = tsend[h]
-    c_land[z] = cb_ref[0]
 
     tail = lax.broadcasted_iota(jnp.int32, (QROWS - hd, codes), 0)
     for slot in range(2):
@@ -113,6 +118,7 @@
         aug[part, :] = jnp.where(lane == 0, hi, jnp.where(lane == 1, mid, jnp.where(lane == 2, low, 0.0))).astype(bf16)
         cols[0:hd, part] = jnp.transpose(c).astype(bf16)
 
+    own_codes.wait()
     prepare(naug.at[0], c_t.at[0], z, 0, codes)
     stat[...] = jnp.full(stat.shape, -3e38, f32)
     q_acc[...] = jnp.zeros(q_acc.shape, f32)
@@ -165,7 +171,7 @@
     def wait_codes(j):
         o = gray(j)
         remote(
-            cb_ref.at[0], c_land.at[lax.rem(z + o, RING)], c_ss.at[3 - o], c_rs.at[3 - o], at_z(4 - o)
+            cb_hbm.at[0], c_land.at[lax.rem(z + o, RING)], c_ss.at[3 - o], c_rs.at[3 - o], at_z(4 - o)
         ).wait_recv()
 
     def stat_copy(b, d):
@@ -175,36 +181,36 @@
     quarter = codes // RING
     logits(0, 0, 0, 0)
 
-    def first_step(p, _):
+    def first_step(p, late):
         @pl.when(p > 0)
         def _():
             wait_rows(p, 1)
 
-        @pl.when(p == 1)
-        def _():
-            for half in range(2):
+        if late:
+            @pl.when(p == 2)
+            def _():
                 for d in (1, 3):
-                    y_copy(d, half).wait_send()
-            for half in range(2):
-                y_copy(2, half).start()
-
-        @pl.when(p == 2)
-        def _():
-            for d in (1, 3):
-                c_copy(d).wait_send()
-            c_copy(2).start()
+                    c_copy(d).wait_send()
+                c_copy(2).start()
+                wait_codes(1)
+        else:
+            @pl.when(p == 1)
+            def _():
+                for half in range(2):
+                    for d in (1, 3):
+                        y_copy(d, half).wait_send()
+                for half in range(2):
+                    y_copy(2, half).start()
 
         logits(0, p, 1, 1)
         finish(0, p, 0, 0)
+        if late:
+            start = pl.multiple_of((p - 2) * (codes // 2), codes // 2)
+            prepare(naug.at[1], c_t.at[1], lax.rem(z + 1, RING), start, codes // 2)
 
         @pl.when(p < RING - 1)
         def _():
             wait_rows(p + 1, 0)
-
-        @pl.when(p == RING - 1)
-        def _():
-            wait_codes(1)
-            prepare(naug.at[1], c_t.at[1], lax.rem(z + 1, RING), 0, codes)
 
         logits((p + 1) // RING, (p + 1) % RING, 0, 0)
         finish(0, p, 1, 1)
@@ -255,7 +261,8 @@
 
         return 0
 
-    lax.fori_loop(0, RING, first_step, 0)
+    lax.fori_loop(0, 2, lambda p, _: first_step(p, False), 0)
+    lax.fori_loop(2, RING, lambda p, _: first_step(p, True), 0)
     lax.fori_loop(RING, pairs, step, 0)
     sum_copy().start()
 
@@ -278,14 +285,17 @@
         for d in range(1, RING):
             total = total + stat_land[d - 1, b, 2:4, :] * jnp.exp2((stat_land[d - 1, b, 0:2, :] - top) * half_log2e)
         inverse = 1.0 / total
-        gain = jnp.exp2((m - top) * half_log2e) * inverse
+        gain[b, 0:2, :] = jnp.exp2((m - top) * half_log2e) * inverse
         even = lax.broadcasted_iota(jnp.int32, (2 * RING, tile), 0) % 2 == 0
         top_all = jnp.where(even, top[0:1, :], top[1:2, :])
         f_buf[b] = jnp.exp2((mloc[b] - top_all) * half_log2e) * jnp.where(even, inverse[0:1, :], inverse[1:2, :])
+
+    def quantized_rows(b):
         for half in range(2):
             cols = slice(half * tile, (half + 1) * tile)
-            qsend[b, :, cols] = (q_acc[2 * b + half, 0:hd, :] * gain[half:half + 1, :]).astype(bf16)
-
+            qsend[b, :, cols] = (q_acc[2 * b + half, 0:hd, :] * gain[b, half:half + 1, :]).astype(bf16)
+
+    def send_rows(b):
         @pl.when(y != b)
         def _():
             q_copy(b).start()
@@ -293,15 +303,16 @@
     def o_copy(d):
         return remote(tsend.at[lax.rem(h + d, heads)], oland.at[h], o_ss.at[d - 1], o_rs.at[d - 1], at_head(d))
 
-    def send_quantized():
-        for d in range(1, RING):
-            q_wait(d).wait()
-        for g in range(heads):
-            cols = slice(g * width, (g + 1) * width)
+    def quantized_part(part):
+        for g in range(heads // 2):
+            head = (heads // 2) * part + g
+            cols = pl.ds(pl.multiple_of(head * width, 128), width)
             block = qsend[y, :, cols].astype(f32)
             for d in range(1, RING):
                 block = block + qland[d - 1, :, cols].astype(f32)
-            tsend[g] = jnp.transpose(block).astype(bf16)
+            tsend[head] = jnp.transpose(block).astype(bf16)
+
+    def send_quantized():
         for d in range(1, heads):
             o_copy(d).start()
         pltpu.make_async_copy(tsend.at[h], oland.at[h], own_sem).start()
@@ -341,12 +352,19 @@
             if jj >= 2:
                 for t in tiles:
                     fetch_copy(base + t).wait()
+            if j == 0 and g == 0:
+                for d in range(1, RING):
+                    q_wait(d).wait()
 
             def some_codes(ch, _, j=j, jj=jj, base=base, tiles=tiles, g=g):
                 part = pl.ds(pl.multiple_of(ch * half_codes, half_codes), half_codes)
                 left = jnp.concatenate([e_buf[base + t, part, :] for t in tiles], axis=1)
                 right = jnp.concatenate([scaled(j, t) for t in tiles], axis=1)
                 out = dot(left, right, 1, 1)
+                if jj == 0:
+                    quantized_rows(2 * g + ch)
+                if j == 0 and g == 0:
+                    quantized_part(ch)
                 if g > 0:
                     out = out + acc[part, :]
                 if g < 2 * RING // group - 1:
@@ -361,14 +379,16 @@
                         k_copy(jj, routes[jj], ch).start()
                     else:
                         acc[part, 0:hd] = out[:, 0:hd]
+                if jj == 0:
+                    send_rows(2 * g + ch)
                 return 0
 
             lax.fori_loop(0, 2, some_codes, 0)
             if jj < 2:
                 for t in tiles:
                     fetch_copy(base + t).start()
-        if jj == 2:
-            send_quantized()
+            if j == 0 and g == 0:
+                send_quantized()
 
     sum_copy().wait()
     book_copies = []
@@ -430,7 +450,7 @@
             jax.ShapeDtypeStruct(ema_sums.shape, f32),
             jax.ShapeDtypeStruct((4 * RING, codes, tile), bf16),
         ),
-        in_specs=[vmem, vmem, vmem, anywhere],
+        in_specs=[anywhere, anywhere, vmem, anywhere],
         out_specs=(anywhere, vmem, anywhere, anywhere),
         scratch_shapes=[
             pltpu.VMEM((4 * RING, codes, tile), bf16),
@@ -441,6 +461,7 @@
             pltpu.VMEM((2, QROWS, codes), bf16),
             pltpu.VMEM((codes, hd), bf16),
             pltpu.VMEM((hd, codes), bf16),
+            pltpu.VMEM(tokens.shape, bf16),
             pltpu.VMEM((heads, hd, width), bf16),
             pltpu.VMEM((RING, hd, rows), bf16),
             pltpu.VMEM((2 * RING, QROWS, tile), f32),
@@ -448,6 +469,7 @@
             pltpu.VMEM((far, RING, 8, tile), f32),
             pltpu.VMEM((RING, 2 * RING, tile), f32),
             pltpu.VMEM((RING, 2 * RING, tile), f32),
+            pltpu.VMEM((RING, 8, tile), f32),
             pltpu.VMEM((RING, hd, rows), bf16),
             pltpu.VMEM((far, hd, rows), bf16),
             pltpu.VMEM((far, codes, hd), bf16),
@@ -457,6 +479,7 @@
             dma((4 * RING,)),
             dma,
             dma,
+            dma((2,)),
             dma((2,)),
             dma((far,)), dma((far,)),
             dma((max(heads - 1, 1),)), dma((max(heads - 1, 1),)),

time: 93 us -> 90.1 us (0.969); the launches traced: 92.9 us -> 88.8 us
  Pallas kernels: 92.2 us -> 88.2 us
    pallas_call x1, Pallas kernels: 89.8 us -> 85.7 us  [shards(): pl.pallas_call(functools.partial(kernel, heads), out_shape=(jax.ShapeDtyp...]
where the time goes in v4:
time: 90.1 us; the launch traced here: 88.8 us
  Pallas kernels  88.2 us (98%)
    pallas_call x1, Pallas kernels, shards(): pl.pallas_call(functools.partial(kernel, heads), out_shape=(jax.ShapeDtyp...  85.7 us
    pallas_call x1, Pallas kernels, shards(): pl.pallas_call(place, out_shape=(jax.ShapeDtypeStruct(tokens.shape, bf16)...  2.46 us

profile of v4, /device:TPU:0, one launch (start us, length us, event | category | flops | bytes accessed | tf_op | source)
XLA Modules:
  0.0 88.8 jit_solution(1375162675806623019)
XLA Ops:
  0.6 85.7 %shard_map.67 = (bf16[8,128,128]{2,1,0:T(8,128)(2,1)}, f32[1,2048]{1,0:T(1,128)}, f32[1,2048,128]{2,1,0:T(8,128)}, bf16[16,2048,512]{2,1,0:T(8,128)(2,1)}) custom-call(bf16[128,1024]{1,0:T(8,128)(2,1)} %tok_hbm.1, bf16[1,2048,128]{2,1,0:T(8,128)(2,1)} %cb_hbm.1, f32[1,2048]{1,0:T(1,128)} %cnt_ref.1, f32[1,2048,128]{2,1,0:T(8,128)} %sums_hbm.1), custom_call_target="tpu_custom_call" | custom-call | tf_op jit(solution)/shard_map/pallas_call | solution.py:445
  86.4 2.5 %shard_map.68 = (bf16[128,1024]{1,0:T(8,128)(2,1)}, f32[1,2048]{1,0:T(1,128)}, f32[1,2048,128]{2,1,0:T(8,128)}) custom-call(bf16[8,128,128]{2,1,0:T(8,128)(2,1)} %get-tuple-element.6.oland, f32[1,2048]{1,0:T(1,128)} %get-tuple-element.7.counts, f32[1,2048,128]{2,1,0:T(8,128)} %get-tuple-element.8.book), custom_call_target="tpu_custom_call" | custom-call | tf_op jit(solution)/shard_map/pallas_call | solution.py:497

commit v5 on v4

--- a/solution.py
+++ b/solution.py
@@ -42,8 +42,13 @@
     codes, hd = cb_hbm.shape[1], cb_hbm.shape[2]
     tile = x_land.shape[2] // 2
 
-    def at_head(d):
-        return (lax.rem(h + d, heads), code)
+    xs = heads // 2
+
+    def from_head(k):
+        return lax.rem(h // 2 + gray(k // 2), xs) * 2 + lax.rem(core + k % 2, 2)
+
+    def to_head(k):
+        return lax.rem(h // 2 + xs - gray(k // 2), xs) * 2 + lax.rem(core + k % 2, 2)
 
     def at_y(d):
         return (h, lax.rem(y + d, RING) * y_step + z * z_step)
@@ -67,8 +72,8 @@
     own_codes.start()
 
     barrier = pltpu.get_barrier_semaphore()
-    for d in range(1, heads):
-        pl.semaphore_signal(barrier, inc=1, device_id=at_head(d), device_id_type=MESH)
+    for k in range(1, heads):
+        pl.semaphore_signal(barrier, inc=1, device_id=(to_head(k), code), device_id_type=MESH)
     for d in range(1, RING):
         pl.semaphore_signal(barrier, inc=1, device_id=at_y(d), device_id_type=MESH)
         pl.semaphore_signal(barrier, inc=1, device_id=at_z(d), device_id_type=MESH)
@@ -78,13 +83,13 @@
         tsend[g] = jnp.transpose(block).astype(bf16)
     pl.semaphore_wait(barrier, heads - 1 + 2 * (RING - 1))
 
-    def head_copy(d):
-        other = lax.rem(h + d, 2)
+    def head_copy(k):
+        head = to_head(k)
+        other = lax.rem(head, 2)
         block = first * (1 - other) + second * other
         return remote(
-            tsend.at[lax.rem(h + d, heads)],
-            x_land.at[block, :, pl.ds(pl.multiple_of(h * width, 128), width)],
-            h_ss.at[d - 1], h_rs.at[d - 1], at_head(d),
+            tsend.at[head], x_land.at[block, :, pl.ds(k * width, width)],
+            h_ss.at[k - 1], h_rs.at[k - 1], (head, code),
         )
 
     def c_copy(d):
@@ -94,11 +99,11 @@
         block = x_land.at[y, :, pl.ds(half * tile, tile)]
         return remote(block, block, y_ss.at[half, d - 1], y_rs.at[half, d - 1], at_y(d))
 
-    for d in range(1, heads):
-        head_copy(d).start()
+    for k in range(1, heads):
+        head_copy(k).start()
     for d in (1, 3):
         c_copy(d).start()
-    x_land[y, :, pl.ds(pl.multiple_of(h * width, 128), width)] = tsend[h]
+    x_land[y, :, 0:width] = tsend[h]
 
     tail = lax.broadcasted_iota(jnp.int32, (QROWS - hd, codes), 0)
     for slot in range(2):
@@ -122,12 +127,6 @@
     prepare(naug.at[0], c_t.at[0], z, 0, codes)
     stat[...] = jnp.full(stat.shape, -3e38, f32)
     q_acc[...] = jnp.zeros(q_acc.shape, f32)
-
-    for d in range(1, heads):
-        head_copy(d).wait()
-    for half in range(2):
-        for d in (1, 3):
-            y_copy(d, half).start()
 
     def row_block(j, s):
         first = 1 - (j + 3) // 4
@@ -179,7 +178,14 @@
 
     pairs = RING * RING
     quarter = codes // RING
-    logits(0, 0, 0, 0)
+
+    for half in range(2):
+        for k in range(max(1, half * heads // 2), (half + 1) * heads // 2):
+            head_copy(k).wait()
+        for d in (1, 3):
+            y_copy(d, half).start()
+        if half == 0:
+            logits(0, 0, 0, 0)
 
     def first_step(p, late):
         @pl.when(p > 0)
@@ -300,36 +306,39 @@
         def _():
             q_copy(b).start()
 
-    def o_copy(d):
-        return remote(tsend.at[lax.rem(h + d, heads)], oland.at[h], o_ss.at[d - 1], o_rs.at[d - 1], at_head(d))
+    def o_copy(k):
+        return remote(tsend.at[k], oland.at[h], o_ss.at[k - 1], o_rs.at[k - 1], (from_head(k), code))
 
     def quantized_part(part):
         for g in range(heads // 2):
-            head = (heads // 2) * part + g
-            cols = pl.ds(pl.multiple_of(head * width, 128), width)
+            k = (heads // 2) * part + g
+            cols = pl.ds(pl.multiple_of(k * width, 128), width)
             block = qsend[y, :, cols].astype(f32)
             for d in range(1, RING):
                 block = block + qland[d - 1, :, cols].astype(f32)
-            tsend[head] = jnp.transpose(block).astype(bf16)
+            tsend[k] = jnp.transpose(block).astype(bf16)
 
     def send_quantized():
-        for d in range(1, heads):
-            o_copy(d).start()
-        pltpu.make_async_copy(tsend.at[h], oland.at[h], own_sem).start()
+        for k in range(1, heads):
+            o_copy(k).start()
+        pltpu.make_async_copy(tsend.at[0], oland.at[h], own_sem).start()
 
     group = 4
     half_codes = codes // 2
     acc = s_buf.at[0, :, pl.ds(0, 2 * hd)]
     pad_row = lax.broadcasted_iota(jnp.int32, (hd, tile), 0)
 
+    def via(d):
+        return at_z(1 if d == 2 else d)
+
     def n_copy(jj, d, ch):
         part = pl.ds(pl.multiple_of(ch * half_codes, half_codes), half_codes)
-        return remote(nsend.at[jj, part], nland.at[d - 1, part], n_ss.at[d - 1, ch], n_rs.at[d - 1, ch], at_z(d))
+        return remote(nsend.at[jj, part], nland.at[d - 1, part], n_ss.at[d - 1, ch], n_rs.at[d - 1, ch], via(d))
 
     def k_copy(jj, d, ch):
         part = pl.ds(pl.multiple_of(ch * half_codes, half_codes), half_codes)
         return remote(
-            ksend.at[jj, :, part], kland.at[d - 1, :, part], k_ss.at[d - 1, ch], k_rs.at[d - 1, ch], at_z(d)
+            ksend.at[jj, :, part], kland.at[d - 1, :, part], k_ss.at[d - 1, ch], k_rs.at[d - 1, ch], via(d)
         )
 
     def scaled(j, t):
@@ -355,6 +364,11 @@
             if j == 0 and g == 0:
                 for d in range(1, RING):
                     q_wait(d).wait()
+
+            if jj == 2 and g > 0:
+                for ch in range(2):
+                    n_copy(0, 2, ch).wait()
+                    k_copy(0, 2, ch).wait()
 
             def some_codes(ch, _, j=j, jj=jj, base=base, tiles=tiles, g=g):
                 part = pl.ds(pl.multiple_of(ch * half_codes, half_codes), half_codes)
@@ -372,13 +386,17 @@
                 else:
                     columns = jnp.transpose(out[:, hd:2 * hd])
                     row = columns[0:1, :] + columns[1:2, :]
+                    numer = out[:, 0:hd]
+                    if jj == 2:
+                        row = row + kland[1, :, part]
+                        numer = numer + nland[1, part, :].astype(f32)
                     ksend[jj, :, part] = row
                     if j > 0:
-                        nsend[jj, part, :] = out[:, 0:hd].astype(bf16)
+                        nsend[jj, part, :] = numer.astype(bf16)
                         n_copy(jj, routes[jj], ch).start()
                         k_copy(jj, routes[jj], ch).start()
                     else:
-                        acc[part, 0:hd] = out[:, 0:hd]
+                        acc[part, 0:hd] = numer
                 if jj == 0:
                     send_rows(2 * g + ch)
                 return 0
@@ -394,12 +412,12 @@
     book_copies = []
     for ch in range(2):
         part = slice(ch * half_codes, (ch + 1) * half_codes)
-        for jj, d in enumerate(routes):
+        for jj, d in ((1, 3), (2, 1)):
             n_copy(jj, d, ch).wait()
             k_copy(jj, d, ch).wait()
         row = ksend[RING - 1, :, part]
         numerators = acc[part, 0:hd]
-        for d in range(1, RING):
+        for d in (1, 3):
             row = row + kland[d - 1, :, part]
             numerators = numerators + nland[d - 1, part, :].astype(f32)
         new_counts = momentum * cnt_ref[:, part] + (1.0 - momentum) * row
@@ -414,9 +432,9 @@
             )
         )
         book_copies[-1].start()
-    for d in range(1, heads):
-        o_copy(d).wait()
-    pltpu.make_async_copy(tsend.at[h], oland.at[h], own_sem).wait()
+    for k in range(1, heads):
+        o_copy(k).wait()
+    pltpu.make_async_copy(tsend.at[0], oland.at[h], own_sem).wait()
     c_copy(2).wait_send()
     for half in range(2):
         y_copy(2, half).wait_send()

time: 90.1 us -> 88.5 us (0.982); the launches traced: 88.8 us -> 88.3 us
  no operation moved by 1% of the time
where the time goes in v5:
time: 88.5 us; the launch traced here: 88.3 us
  Pallas kernels  87.7 us (99%)
    pallas_call x1, Pallas kernels, shards(): pl.pallas_call(functools.partial(kernel, heads), out_shape=(jax.ShapeDtyp...  85.2 us
    pallas_call x1, Pallas kernels, shards(): pl.pallas_call(place, out_shape=(jax.ShapeDtypeStruct(tokens.shape, bf16)...  2.46 us

profile of v5, /device:TPU:0, one launch (start us, length us, event | category | flops | bytes accessed | tf_op | source)
XLA Modules:
  0.0 88.3 jit_solution(100709309381194271)
XLA Ops:
  0.6 85.2 %shard_map.67 = (bf16[8,128,128]{2,1,0:T(8,128)(2,1)}, f32[1,2048]{1,0:T(1,128)}, f32[1,2048,128]{2,1,0:T(8,128)}, bf16[16,2048,512]{2,1,0:T(8,128)(2,1)}) custom-call(bf16[128,1024]{1,0:T(8,128)(2,1)} %tok_hbm.1, bf16[1,2048,128]{2,1,0:T(8,128)(2,1)} %cb_hbm.1, f32[1,2048]{1,0:T(1,128)} %cnt_ref.1, f32[1,2048,128]{2,1,0:T(8,128)} %sums_hbm.1), custom_call_target="tpu_custom_call" | custom-call | tf_op jit(solution)/shard_map/pallas_call | solution.py:463
  85.9 2.5 %shard_map.68 = (bf16[128,1024]{1,0:T(8,128)(2,1)}, f32[1,2048]{1,0:T(1,128)}, f32[1,2048,128]{2,1,0:T(8,128)}) custom-call(bf16[8,128,128]{2,1,0:T(8,128)(2,1)} %get-tuple-element.6.oland, f32[1,2048]{1,0:T(1,128)} %get-tuple-element.7.counts, f32[1,2048,128]{2,1,0:T(8,128)} %get-tuple-element.8.book), custom_call_target="tpu_custom_call" | custom-call | tf_op jit(solution)/shard_map/pallas_call | solution.py:515

commit v6 on v5

--- a/solution.py
+++ b/solution.py
@@ -186,6 +186,8 @@
             y_copy(d, half).start()
         if half == 0:
             logits(0, 0, 0, 0)
+    for half in range(2):
+        y_copy(2, half).start()
 
     def first_step(p, late):
         @pl.when(p > 0)
@@ -199,14 +201,6 @@
                     c_copy(d).wait_send()
                 c_copy(2).start()
                 wait_codes(1)
-        else:
-            @pl.when(p == 1)
-            def _():
-                for half in range(2):
-                    for d in (1, 3):
-                        y_copy(d, half).wait_send()
-                for half in range(2):
-                    y_copy(2, half).start()
 
         logits(0, p, 1, 1)
         finish(0, p, 0, 0)
@@ -365,6 +359,10 @@
                 for d in range(1, RING):
                     q_wait(d).wait()
 
+            if j == 0 and g > 0:
+                for ch in range(2):
+                    n_copy(1, 3, ch).wait()
+                    k_copy(1, 3, ch).wait()
             if jj == 2 and g > 0:
                 for ch in range(2):
                     n_copy(0, 2, ch).wait()
@@ -387,9 +385,9 @@
                     columns = jnp.transpose(out[:, hd:2 * hd])
                     row = columns[0:1, :] + columns[1:2, :]
                     numer = out[:, 0:hd]
-                    if jj == 2:
-                        row = row + kland[1, :, part]
-                        numer = numer + nland[1, part, :].astype(f32)
+                    if jj >= 2:
+                        row = row + kland[jj - 1, :, part]
+                        numer = numer + nland[jj - 1, part, :].astype(f32)
                     ksend[jj, :, part] = row
                     if j > 0:
                         nsend[jj, part, :] = numer.astype(bf16)
@@ -412,14 +410,10 @@
     book_copies = []
     for ch in range(2):
         part = slice(ch * half_codes, (ch + 1) * half_codes)
-        for jj, d in ((1, 3), (2, 1)):
-            n_copy(jj, d, ch).wait()
-            k_copy(jj, d, ch).wait()
-        row = ksend[RING - 1, :, part]
-        numerators = acc[part, 0:hd]
-        for d in (1, 3):
-            row = row + kland[d - 1, :, part]
-            numerators = numerators + nland[d - 1, part, :].astype(f32)
+        n_copy(2, 1, ch).wait()
+        k_copy(2, 1, ch).wait()
+        row = ksend[RING - 1, :, part] + kland[0, :, part]
+        numerators = acc[part, 0:hd] + nland[0, part, :].astype(f32)
         new_counts = momentum * cnt_ref[:, part] + (1.0 - momentum) * row
         ncnt_ref[:, part] = new_counts
         inverse_counts = jnp.transpose(jnp.broadcast_to(1.0 / new_counts, (8, half_codes)))[:, 0:1]
@@ -437,7 +431,8 @@
     pltpu.make_async_copy(tsend.at[0], oland.at[h], own_sem).wait()
     c_copy(2).wait_send()
     for half in range(2):
-        y_copy(2, half).wait_send()
+        for d in range(1, RING):
+            y_copy(d, half).wait_send()
     for copy in book_copies:
         copy.wait()
 
@@ -519,8 +514,17 @@
             jax.ShapeDtypeStruct(ema_counts.shape, f32),
             jax.ShapeDtypeStruct(ema_sums.shape, f32),
         ),
-        in_specs=[vmem] * 3,
-        out_specs=(vmem,) * 3,
+        grid=(2,),
+        in_specs=[
+            pl.BlockSpec((heads // 2, width, hd), lambda i: (i, 0, 0)),
+            pl.BlockSpec((1, codes // 2), lambda i: (0, i)),
+            pl.BlockSpec((1, codes // 2, hd), lambda i: (0, i, 0)),
+        ],
+        out_specs=(
+            pl.BlockSpec((width, heads // 2 * hd), lambda i: (0, i)),
+            pl.BlockSpec((1, codes // 2), lambda i: (0, i)),
+            pl.BlockSpec((1, codes // 2, hd), lambda i: (0, i, 0)),
+        ),
     )(pieces, counts, book)
 
 

time: 88.5 us -> 87.5 us (0.989)
  Pallas kernels: 87.7 us -> 86.7 us
where the time goes in v6:
time: 87.5 us; the launch traced here: 87.3 us
  Pallas kernels  86.7 us (99%)
    pallas_call x1, Pallas kernels, shards(): pl.pallas_call(functools.partial(kernel, heads), out_shape=(jax.ShapeDtyp...  84.5 us
    pallas_call x1, Pallas kernels, shards(): pl.pallas_call(place, out_shape=(jax.ShapeDtypeStruct(tokens.shape, bf16)...  2.25 us

profile of v6, /device:TPU:0, one launch (start us, length us, event | category | flops | bytes accessed | tf_op | source)
XLA Modules:
  0.0 87.3 jit_solution(13150783779564713900)
XLA Ops:
  0.6 84.5 %shard_map.67 = (bf16[8,128,128]{2,1,0:T(8,128)(2,1)}, f32[1,2048]{1,0:T(1,128)}, f32[1,2048,128]{2,1,0:T(8,128)}, bf16[16,2048,512]{2,1,0:T(8,128)(2,1)}) custom-call(bf16[128,1024]{1,0:T(8,128)(2,1)} %tok_hbm.1, bf16[1,2048,128]{2,1,0:T(8,128)(2,1)} %cb_hbm.1, f32[1,2048]{1,0:T(1,128)} %cnt_ref.1, f32[1,2048,128]{2,1,0:T(8,128)} %sums_hbm.1), custom_call_target="tpu_custom_call" | custom-call | tf_op jit(solution)/shard_map/pallas_call | solution.py:458
  85.1 2.3 %shard_map.68 = (bf16[128,1024]{1,0:T(8,128)(2,1)}, f32[1,2048]{1,0:T(1,128)}, f32[1,2048,128]{2,1,0:T(8,128)}) custom-call(bf16[8,128,128]{2,1,0:T(8,128)(2,1)} %get-tuple-element.6.oland, f32[1,2048]{1,0:T(1,128)} %get-tuple-element.7.counts, f32[1,2048,128]{2,1,0:T(8,128)} %get-tuple-element.8.book), custom_call_target="tpu_custom_call" | custom-call | tf_op jit(solution)/shard_map/pallas_call | solution.py:510
